TPU v7x, 512 devices: a whole 4x4x16 slice. The times are simulated.
512 devices in a mesh: dp: 4 (over x), ctx: 16 (over z_lo, y), section: 8 (over z_hi, core).
Axes of the slice: x: 4, y: 4, z: 16 (z_hi: 4, z_lo: 4; z = z_hi * 4 + z_lo), core: 2. Of those that a mesh axis runs over, the one named last changes fastest.
Arguments:
- queries: bfloat16 [4, 8, 2048, 4096], P('dp', 'section', 'ctx'), may hold values from -20 to 20
- keys: bfloat16 [4, 8, 2048, 512], P('dp', 'section', 'ctx'), may hold values from -20 to 20
- values: bfloat16 [4, 8, 2048, 512], P('dp', 'section', 'ctx'), may hold values from -6 to 6
- out_grad: bfloat16 [4, 8, 2048, 4096], P('dp', 'section', 'ctx'), may hold values from -6 to 6
- send_slot: int32 [4, 4], replicated, may hold values from 0 to 3, each once within a row
- recv_slot: int32 [4, 4], replicated, may hold values from 0 to 3, each once within a row
- stretch_block: int32 [4, 8, 64], P('dp', 'section'), may hold values from 0 to 63, each once within a row
- doc_ids: int32 [4, 8, 2048], P('dp', 'section'), may hold values from 0 to 31, never falling along the last dimension, each value on 1 to 96 neighbouring positions
Outputs:
- handoff: bfloat16 [4, 8, 2048, 4096], P('dp', 'section', 'ctx')
- query_grad: bfloat16 [4, 8, 2048, 4096], P('dp', 'section', 'ctx')
- key_gradient: bfloat16 [4, 8, 2048, 512], P('dp', 'section', 'ctx')
- value_gradient: bfloat16 [4, 8, 2048, 512], P('dp', 'section', 'ctx')
Inputs may be any that keep to these rules, and one draw needn't show every extreme that they name: `send_slot`: each row is a permutation of the replicas' block indices. `recv_slot`: each row is a permutation of the replicas' block indices. `stretch_block`: each sequence's row is a permutation of its 64 position blocks. `doc_ids`: documents are contiguous runs of positions, numbered in order, none longer than 96.
All inputs are finite; a program needn't handle non-finite values.
Results may differ from a plain program's by a relative error of at most 0.025.
Values may be sent and summed in bfloat16 or wider, within the bound.
No kernel may reach another device: no remote copies, remote signals or barrier semaphores. Data moves between devices by JAX's collectives and lax.ppermute only.
A program may use at most 64 MiB of HBM per device.

v0:
```python
import jax
import jax.numpy as jnp
from jax import lax
from jax.sharding import PartitionSpec as P

QUERY_HEADS = 32
KEY_VALUE_HEADS = 4
HEAD_SIZE = 128
BLOCK_POSITIONS = 32
REACH_BLOCKS = 4


def from_behind(block, axis, distance):
    devices = range(lax.axis_size(axis))
    route = [((i - distance) % len(devices), i) for i in devices]
    return lax.ppermute(block, axis, route)


def inverse_table(table, count):
    numbers = jnp.arange(count, dtype=jnp.int32)
    return jnp.sum(jnp.where(table[None, :] == numbers[:, None], numbers[None, :], 0), axis=1)


def route_blocks(tensor, send_order):
    pieces = send_order.shape[0]
    row_count = tensor.shape[0]
    row_width = tensor.shape[-1]
    return jnp.take(
        tensor.reshape(pieces, row_count // pieces, row_width), send_order, axis=0
    ).reshape(row_count, row_width)


def attend_forward(query_fresh, key_complete, value_complete, stretch_row, doc_row, me_ctx):
    tok_rows = query_fresh.shape[0]
    device_share = tok_rows // BLOCK_POSITIONS
    nblocks = stretch_row.shape[0]
    head_group = QUERY_HEADS // KEY_VALUE_HEADS
    scale = HEAD_SIZE ** (-0.5)
    slot_of = inverse_table(stretch_row, nblocks)
    mine = lax.dynamic_slice_in_dim(stretch_row, me_ctx * device_share, device_share)
    firsts = jnp.clip(mine - (REACH_BLOCKS - 1), 0, nblocks - REACH_BLOCKS)
    win_blocks = firsts[:, None] + jnp.arange(REACH_BLOCKS, dtype=jnp.int32)[None, :]
    offsets = jnp.arange(BLOCK_POSITIONS, dtype=jnp.int32)
    key_row_list = (jnp.take(slot_of, win_blocks)[:, :, None] * BLOCK_POSITIONS + offsets).reshape(
        device_share, REACH_BLOCKS * BLOCK_POSITIONS
    )
    key_at = (win_blocks[:, :, None] * BLOCK_POSITIONS + offsets).reshape(
        device_share, REACH_BLOCKS * BLOCK_POSITIONS
    )
    query_at = mine[:, None] * BLOCK_POSITIONS + offsets[None, :]
    allowed = (jnp.take(doc_row, key_at)[:, None, :] == jnp.take(doc_row, query_at)[:, :, None]) & (
        key_at[:, None, :] <= query_at[:, :, None]
    )
    mask_five = allowed[:, None, None, :, :]
    query_five = query_fresh.reshape(
        device_share, BLOCK_POSITIONS, KEY_VALUE_HEADS, head_group, HEAD_SIZE
    )
    key_four = jnp.take(key_complete, key_row_list, axis=0).reshape(
        device_share, REACH_BLOCKS * BLOCK_POSITIONS, KEY_VALUE_HEADS, HEAD_SIZE
    )
    value_four = jnp.take(value_complete, key_row_list, axis=0).reshape(
        device_share, REACH_BLOCKS * BLOCK_POSITIONS, KEY_VALUE_HEADS, HEAD_SIZE
    )
    logits = (
        jnp.einsum("tqhgd,tkhd->thgqk", query_five, key_four, preferred_element_type=jnp.float32)
        * scale
    )
    logits = jnp.where(mask_five, logits, -1e30)
    peak = jnp.max(logits, axis=-1, keepdims=True)
    weights = jnp.where(mask_five, jnp.exp(logits - peak), 0.0)
    probs = weights / jnp.sum(weights, axis=-1, keepdims=True)
    probs_low = probs.astype(jnp.bfloat16)
    attn = jnp.einsum(
        "thgqk,tkhd->tqhgd", probs_low, value_four, preferred_element_type=jnp.float32
    ).astype(jnp.bfloat16)
    return (attn, probs, probs_low, query_five, key_four, value_four, key_row_list)


def attend_backward(
    gradient_fresh,
    attn,
    probs,
    probs_low,
    query_five,
    key_four,
    value_four,
    key_row_list,
    dense_rows,
):
    tok_rows = gradient_fresh.shape[0]
    device_share = tok_rows // BLOCK_POSITIONS
    head_group = QUERY_HEADS // KEY_VALUE_HEADS
    scale = HEAD_SIZE ** (-0.5)
    gradient_five = gradient_fresh.reshape(
        device_share, BLOCK_POSITIONS, KEY_VALUE_HEADS, head_group, HEAD_SIZE
    )
    delta = jnp.einsum("tqhgd,tqhgd->thgq", gradient_five, attn, preferred_element_type=jnp.float32)
    dprob = jnp.einsum(
        "tqhgd,tkhd->thgqk", gradient_five, value_four, preferred_element_type=jnp.float32
    )
    dlogit = (probs * (dprob - delta[..., None])).astype(jnp.bfloat16)
    q_grad = (
        jnp.einsum("thgqk,tkhd->tqhgd", dlogit, key_four, preferred_element_type=jnp.float32)
        * scale
    ).astype(jnp.bfloat16)
    key_summands = (
        jnp.einsum("thgqk,tqhgd->tkhd", dlogit, query_five, preferred_element_type=jnp.float32)
        * scale
    )
    value_summands = jnp.einsum(
        "thgqk,tqhgd->tkhd", probs_low, gradient_five, preferred_element_type=jnp.float32
    )
    flat_rows = key_row_list.reshape(-1)
    key_value_width = KEY_VALUE_HEADS * HEAD_SIZE
    k_dense = (
        jnp.zeros((dense_rows, key_value_width), jnp.float32)
        .at[flat_rows]
        .add(key_summands.reshape(-1, key_value_width))
    )
    v_dense = (
        jnp.zeros((dense_rows, key_value_width), jnp.float32)
        .at[flat_rows]
        .add(value_summands.reshape(-1, key_value_width))
    )
    k_mine, v_mine = (
        lax.psum_scatter(
            k_dense.astype(jnp.bfloat16), "ctx", scatter_dimension=0, tiled=True
        ).astype(jnp.float32),
        lax.psum_scatter(
            v_dense.astype(jnp.bfloat16), "ctx", scatter_dimension=0, tiled=True
        ).astype(jnp.float32),
    )
    return (
        q_grad.reshape(tok_rows, QUERY_HEADS * HEAD_SIZE),
        k_mine.astype(jnp.bfloat16),
        v_mine.astype(jnp.bfloat16),
    )


def on_device(queries, keys, values, out_grad, send_slot, recv_slot, stretch_block, doc_ids):
    dp_count = lax.axis_size("dp")
    me_dp = lax.axis_index("dp")
    me_ctx = lax.axis_index("ctx")
    q_rows = queries[0, 0]
    k_rows = keys[0, 0]
    v_rows = values[0, 0]
    g_rows = out_grad[0, 0]
    tok_rows = q_rows.shape[0]
    key_value_width = k_rows.shape[1]
    send_order = jnp.take(send_slot, me_dp, axis=0)
    arrival = inverse_table(jnp.take(recv_slot, me_dp, axis=0), dp_count)
    query_fresh, k_new, v_new, gradient_fresh = (
        lax.all_to_all(
            route_blocks(q_rows, send_order), "dp", split_axis=0, concat_axis=0, tiled=True
        ),
        lax.all_to_all(
            route_blocks(k_rows, send_order), "dp", split_axis=0, concat_axis=0, tiled=True
        ),
        lax.all_to_all(
            route_blocks(v_rows, send_order), "dp", split_axis=0, concat_axis=0, tiled=True
        ),
        lax.all_to_all(
            route_blocks(g_rows, send_order), "dp", split_axis=0, concat_axis=0, tiled=True
        ),
    )
    query_fresh = route_blocks(query_fresh, arrival)
    gradient_fresh = route_blocks(gradient_fresh, arrival)
    key_complete, value_complete = (
        lax.all_gather(route_blocks(k_new, arrival), "ctx", axis=0, tiled=True),
        lax.all_gather(route_blocks(v_new, arrival), "ctx", axis=0, tiled=True),
    )
    stretch_row = stretch_block[0, 0]
    doc_row = doc_ids[0, 0]
    attn, probs, probs_low, query_five, key_four, value_four, key_row_list = attend_forward(
        query_fresh, key_complete, value_complete, stretch_row, doc_row, me_ctx
    )
    attn_rows = attn.reshape(tok_rows, QUERY_HEADS * HEAD_SIZE)
    q_grad, k_grad, v_grad = attend_backward(
        gradient_fresh,
        attn,
        probs,
        probs_low,
        query_five,
        key_four,
        value_four,
        key_row_list,
        key_complete.shape[0],
    )
    handoff = from_behind(attn_rows, "section", 1)
    return (
        handoff.reshape(1, 1, tok_rows, QUERY_HEADS * HEAD_SIZE),
        q_grad.reshape(1, 1, tok_rows, QUERY_HEADS * HEAD_SIZE),
        k_grad.reshape(1, 1, tok_rows, key_value_width),
        v_grad.reshape(1, 1, tok_rows, key_value_width),
    )


def solution(mesh):
    placed = (
        P("dp", "section", "ctx", None),
        P("dp", "section", "ctx", None),
        P("dp", "section", "ctx", None),
        P("dp", "section", "ctx", None),
        P(),
        P(),
        P("dp", "section", None),
        P("dp", "section", None),
    )
    return jax.shard_map(
        on_device,
        mesh=mesh,
        in_specs=placed,
        out_specs=(
            P("dp", "section", "ctx", None),
            P("dp", "section", "ctx", None),
            P("dp", "section", "ctx", None),
            P("dp", "section", "ctx", None),
        ),
        check_vma=False,
    )
```

profile of v0, /device:TPU:2, one launch (start us, length us, event | category | flops | bytes accessed | tf_op | source)
XLA Modules:
  0.0 468.5 jit_solution(5305136093989905155)
XLA Ops:
  11.7 9.2 %all-to-all-start.1 = ((bf16[4,32,512]{2,1,0:T(8,128)(2,1)}), bf16[4,32,512]{2,1,0:T(8,128)(2,1)S(1)}, u32[]{:S(2)}, u32[]{:S(2)}) async-start(bf16[4,32,512]{2,1,0:T(8,128)(2,1)} %get-tuple-element.31), calls=%async_computation.1 | async-start | bytes 262144 | tf_op jit(solution)/shard_map/all_to_all | solution.py:156
  21.7 3.7 all-to-all-done.1
  25.4 4.8 %all-to-all-start = ((bf16[4,32,512]{2,1,0:T(8,128)(2,1)}), bf16[4,32,512]{2,1,0:T(8,128)(2,1)S(1)}, u32[]{:S(2)}, u32[]{:S(2)}) async-start(bf16[4,32,512]{2,1,0:T(8,128)(2,1)} %get-tuple-element.32), calls=%async_computation | async-start | bytes 262144 | tf_op jit(solution)/shard_map/all_to_all | solution.py:159
  30.8 3.9 all-to-all-done
  40.1 5.1 %all-to-all-start.3 = ((bf16[4,32,4096]{2,1,0:T(8,128)(2,1)}), bf16[4,32,4096]{2,1,0:T(8,128)(2,1)S(1)}, u32[]{:S(2)}, u32[]{:S(2)}) async-start(bf16[4,32,4096]{2,1,0:T(8,128)(2,1)} %get-tuple-element.25), calls=%async_computation.3 | async-start | bytes 2097152 | tf_op jit(solution)/shard_map/all_to_all | solution.py:162
  47.7 3.1 gather_fusion.1
  51.0 3.7 all-to-all-done.3
  54.7 5.7 %all-to-all-start.2 = ((bf16[4,32,4096]{2,1,0:T(8,128)(2,1)}), bf16[4,32,4096]{2,1,0:T(8,128)(2,1)}, u32[]{:S(2)}, u32[]{:S(2)}) async-start(bf16[4,32,4096]{2,1,0:T(8,128)(2,1)} %get-tuple-element.26), calls=%async_computation.2 | async-start | bytes 2097152 | tf_op jit(solution)/shard_map/all_to_all | solution.py:153
  62.5 7.4 %all-to-all-done.2 = bf16[4,32,4096]{2,1,0:T(8,128)(2,1)} async-done(((bf16[4,32,4096]{2,1,0:T(8,128)(2,1)}), bf16[4,32,4096]{2,1,0:T(8,128)(2,1)}, u32[]{:S(2)}, u32[]{:S(2)}) %all-to-all-start.2) | async-done | bytes 1048608 | tf_op jit(solution)/shard_map/all_to_all | solution.py:153
  73.9 49.7 %all-gather.3.cloned.1.call-done = bf16[2048,512]{1,0:T(8,128)(2,1)} async-done(((bf16[128,512]{1,0:T(8,128)(2,1)}), bf16[2048,512]{1,0:T(8,128)(2,1)}) %all-gather.3.cloned.1.call-update) | async-done | bytes 2097168 | tf_op jit(solution)/shard_map/all_gather | solution.py:170
  123.6 4.5 gather_fusion.5
  130.1 83.1 %all-gather.5.cloned.1.call-done = bf16[2048,512]{1,0:T(8,128)(2,1)} async-done(((bf16[128,512]{1,0:T(8,128)(2,1)}), bf16[2048,512]{1,0:T(8,128)(2,1)}) %all-gather.5.cloned.1.call-update) | async-done | bytes 2097168 | tf_op jit(solution)/shard_map/all_gather | solution.py:169
  213.2 4.5 gather_fusion.8
  219.8 2.3 broadcast_select_fusion.4
  222.1 3.8 fusion.42
  227.9 2.5 multiply_reduce_fusion
  233.9 5.8 %scatter_custom_fusion = f32[2048,512]{1,0:T(8,128)} fusion(s32[512]{0:T(512)S(1)} %bitcast.135, f32[]{:T(128)} %constant.93.clone.1, f32[64,8,4,128]{3,2,1,0:T(4,128)S(1)} %bitcast.121), kind=kCustom, calls=%fused_computation.23 | custom fusion | flops 262144 | bytes 5242884 | tf_op jit(solution)/shard_map/scatter-add | solution.py:118
  239.7 3.8 convert_element_type.34
  248.2 5.8 %scatter_custom_fusion.1 = f32[2048,512]{1,0:T(8,128)} fusion(s32[512]{0:T(512)S(1)} %bitcast.136, f32[]{:T(128)} %constant.93.clone.1, f32[64,8,4,128]{3,2,1,0:T(4,128)S(1)} %bitcast.120), kind=kCustom, calls=%fused_computation.21 | custom fusion | flops 262144 | bytes 5242884 | tf_op jit(solution)/shard_map/scatter-add | solution.py:123
  254.1 3.8 convert_element_type.35
  266.1 50.6 %collective-permute-done = bf16[128,4096]{1,0:T(8,128)(2,1)} collective-permute-done((bf16[128,4096]{1,0:T(8,128)(2,1)}, bf16[128,4096]{1,0:T(8,128)(2,1)}, u32[]{:S(2)}, u32[]{:S(2)}) %collective-permute-start) | collective-permute-done | bytes 1048608 | tf_op jit(solution)/shard_map/ppermute | solution.py:16
  316.7 48.3 %reduce-scatter.3.cloned.1.call-done = bf16[128,512]{1,0:T(8,128)(2,1)} async-done(((bf16[2048,512]{1,0:T(8,128)(2,1)}), bf16[128,512]{1,0:T(8,128)(2,1)}) %reduce-scatter.3.cloned.1.call-update) | async-done | bytes 131088 | tf_op jit(solution)/shard_map/reduce_scatter | solution.py:126
  365.0 94.6 %reduce-scatter.5.cloned.1.call-done = bf16[128,512]{1,0:T(8,128)(2,1)} async-done(((bf16[2048,512]{1,0:T(8,128)(2,1)}), bf16[128,512]{1,0:T(8,128)(2,1)}) %reduce-scatter.5.cloned.1.call-update) | async-done | bytes 131088 | tf_op jit(solution)/shard_map/reduce_scatter | solution.py:129
  459.7 2.3 copy.96
  (102 shorter events, 42.3 us)
Async XLA Ops:
  7.2 28.9 %copy-start = (bf16[1,1,128,4096]{3,2,1,0:T(8,128)(2,1)S(1)}, bf16[1,1,128,4096]{3,2,1,0:T(8,128)(2,1)}, u32[]{:S(2)}) copy-start(bf16[1,1,128,4096]{3,2,1,0:T(8,128)(2,1)} %param.19) | copy-start | bytes 3145732
  11.7 13.7 %all-to-all-start.1 = ((bf16[4,32,512]{2,1,0:T(8,128)(2,1)}), bf16[4,32,512]{2,1,0:T(8,128)(2,1)S(1)}, u32[]{:S(2)}, u32[]{:S(2)}) async-start(bf16[4,32,512]{2,1,0:T(8,128)(2,1)} %get-tuple-element.31), calls=%async_computation.1 | async-start | bytes 262144 | tf_op jit(solution)/shard_map/all_to_all | solution.py:156
  25.4 9.3 %all-to-all-start = ((bf16[4,32,512]{2,1,0:T(8,128)(2,1)}), bf16[4,32,512]{2,1,0:T(8,128)(2,1)S(1)}, u32[]{:S(2)}, u32[]{:S(2)}) async-start(bf16[4,32,512]{2,1,0:T(8,128)(2,1)} %get-tuple-element.32), calls=%async_computation | async-start | bytes 262144 | tf_op jit(solution)/shard_map/all_to_all | solution.py:159
  30.2 93.4 %all-gather.3.cloned.1.call-start = ((), (), s32[]{:S(2)}) async-start(), calls=%async_computation.6 | async-start | bytes 2228224 | tf_op jit(solution)/shard_map/all_gather | solution.py:170
  40.1 5.1 %copy-start.13 = (s32[1,1,64]{2,1,0:T(1,128)S(1)}, s32[1,1,64]{2,1,0:T(1,128)}, u32[]{:S(2)}) copy-start(s32[1,1,64]{2,1,0:T(1,128)} %param.22) | copy-start | bytes 772
  40.1 7.6 %copy-start.1 = (s32[1,1,2048]{2,1,0:T(1,128)S(1)}, s32[1,1,2048]{2,1,0:T(1,128)}, u32[]{:S(2)}) copy-start(s32[1,1,2048]{2,1,0:T(1,128)} %param.23) | copy-start | bytes 24580
  40.1 14.5 %all-to-all-start.3 = ((bf16[4,32,4096]{2,1,0:T(8,128)(2,1)}), bf16[4,32,4096]{2,1,0:T(8,128)(2,1)S(1)}, u32[]{:S(2)}, u32[]{:S(2)}) async-start(bf16[4,32,4096]{2,1,0:T(8,128)(2,1)} %get-tuple-element.25), calls=%async_computation.3 | async-start | bytes 2097152 | tf_op jit(solution)/shard_map/all_to_all | solution.py:162
  45.2 168.0 %all-gather.5.cloned.1.call-start = ((), (), s32[]{:S(2)}) async-start(), calls=%async_computation.7 | async-start | bytes 2228224 | tf_op jit(solution)/shard_map/all_gather | solution.py:169
  54.7 15.2 %all-to-all-start.2 = ((bf16[4,32,4096]{2,1,0:T(8,128)(2,1)}), bf16[4,32,4096]{2,1,0:T(8,128)(2,1)}, u32[]{:S(2)}, u32[]{:S(2)}) async-start(bf16[4,32,4096]{2,1,0:T(8,128)(2,1)} %get-tuple-element.26), calls=%async_computation.2 | async-start | bytes 2097152 | tf_op jit(solution)/shard_map/all_to_all | solution.py:153
  60.3 304.7 %reduce-scatter.3.cloned.1.call-start = ((), (), s32[]{:S(2)}) async-start(), calls=%async_computation.8 | async-start | bytes 2228224 | tf_op jit(solution)/shard_map/reduce_scatter | solution.py:126
  72.3 1.3 copy-start.2
  225.9 2.0 copy-start.9
  227.9 2.5 copy-start.5
  227.9 2.5 copy-start.3
  227.9 2.5 copy-start.10
  230.4 2.4 copy-start.12
  231.7 1.1 copy-start.11
  243.5 1.2 copy-start.4
  243.5 1.5 copy-start.6
  243.5 216.2 %reduce-scatter.5.cloned.1.call-start = ((), (), s32[]{:S(2)}) async-start(), calls=%async_computation.9 | async-start | bytes 2228224 | tf_op jit(solution)/shard_map/reduce_scatter | solution.py:129
  257.9 1.2 copy-start.7
  259.5 3.2 copy-start.8
  260.8 55.9 %collective-permute-start = (bf16[128,4096]{1,0:T(8,128)(2,1)}, bf16[128,4096]{1,0:T(8,128)(2,1)}, u32[]{:S(2)}, u32[]{:S(2)}) collective-permute-start(bf16[128,4096]{1,0:T(8,128)(2,1)} %reshape.431), channel_id=1, source_target_pairs={{7,0},{0,1},{1,2},{2,3},{3,4},{4,5},{5,6},{6,7},{15,8},{8,9},{9,10... | collective-permute-start | bytes 3145736 | tf_op jit(solution)/shard_map/ppermute | solution.py:16
Sparse Core Ops, SparseCore 0:
  36.2 87.3 all-gather.2
  126.2 86.9 all-gather.4
  243.6 121.3 reduce-scatter.2
  368.3 91.3 reduce-scatter.4
where the time goes:
time: 470 us; the launch traced here: 468 us
  waiting for transfers between devices  346 us (74%)
  local copies, waits for them, and re-layouts  40.9 us (9%)
  other arithmetic  29.5 us (6%)
  starting transfers between devices  26.6 us (6%)
  between operations  14.1 us (3%)
  matrix products  11.5 us (2%)
    reduce_scatter x1, waiting for transfers between devices, attend_backward(): lax.psum_scatter(v_dense.astype(jnp.bfloat16), 'ctx', scatter_dimension=0...  94.6 us
    all_gather x1, waiting for transfers between devices, on_device(): lax.all_gather(route_blocks(k_new, arrival), 'ctx', axis=0, tiled=True)  83.1 us
    ppermute x1, waiting for transfers between devices, from_behind(): return lax.ppermute(block, axis, route)  50.6 us
    all_gather x1, waiting for transfers between devices, on_device(): lax.all_gather(route_blocks(v_new, arrival), 'ctx', axis=0, tiled=True)  49.7 us
    reduce_scatter x1, waiting for transfers between devices, attend_backward(): lax.psum_scatter(k_dense.astype(jnp.bfloat16), 'ctx', scatter_dimension=0...  48.3 us
  transfers between devices with their start and end apart: 9, of which 9 were waited for; matrix products, arithmetic and copies ran while one was open for 9% of the time, Pallas kernels for 0%

commit v1 on v0

v1 whole, which is shorter than its diff:
```python
import jax
import jax.numpy as jnp
from jax import lax
from jax.experimental import pallas as pl
from jax.experimental.pallas import tpu as pltpu
from jax.sharding import PartitionSpec as P

QUERY_HEADS = 32
KEY_VALUE_HEADS = 4
HEAD_SIZE = 128
BLOCK_POSITIONS = 32
N_DP = 4
N_CTX = 16
NB = 64
GROUP = QUERY_HEADS // KEY_VALUE_HEADS
QW = QUERY_HEADS * HEAD_SIZE
KW = KEY_VALUE_HEADS * HEAD_SIZE
G_AT = QW
K_AT = 2 * QW
V_AT = 2 * QW + KW
PAYLOAD = 2 * QW + 2 * KW
HALF = BLOCK_POSITIONS // 2
BEHIND = 3
ENTRIES = N_DP * BEHIND
SCALE = HEAD_SIZE ** (-0.5)

VMEM = pl.BlockSpec(memory_space=pltpu.VMEM)
SMEM = pl.BlockSpec(memory_space=pltpu.SMEM)


def call(kernel, out_shape, in_specs, scratch=(), flops=0, nbytes=1 << 20):
    multi = isinstance(out_shape, (list, tuple))
    return pl.pallas_call(
        kernel,
        out_shape=out_shape,
        in_specs=in_specs,
        out_specs=[VMEM] * len(out_shape) if multi else VMEM,
        scratch_shapes=scratch,
        compiler_params=pltpu.CompilerParams(vmem_limit_bytes=40 * 1024 * 1024),
        cost_estimate=pl.CostEstimate(flops=flops, bytes_accessed=nbytes, transcendentals=0),
    )


def bf16(*shape):
    return jax.ShapeDtypeStruct(shape, jnp.bfloat16)


def replica(me, shift):
    return lax.rem(me + shift + N_DP, N_DP)


def rows(block, half=0, count=BLOCK_POSITIONS):
    return pl.ds(pl.multiple_of(block * BLOCK_POSITIONS + half * HALF, HALF), count)


def pack_kv(me, send, k_ref, v_ref, out_ref):
    r = me[0]
    for u in range(N_DP):
        block = send[r, u]
        for piece in range(N_CTX):
            head, half = piece // 2, piece % 2
            source = k_ref if head < KEY_VALUE_HEADS else v_ref
            column = (head % KEY_VALUE_HEADS) * HEAD_SIZE
            out_ref[u * N_CTX + piece] = source[
                rows(block, half, HALF), column : column + HEAD_SIZE
            ]


def pack_rows(me, send, q_ref, g_ref, k_ref, v_ref, *outs):
    r = me[0]
    for shift in range(N_DP):
        block = send[r, replica(r, shift)]
        outs[shift][:, :G_AT] = q_ref[rows(block), :]
        outs[shift][:, G_AT:K_AT] = g_ref[rows(block), :]
        outs[shift][:, K_AT:V_AT] = k_ref[rows(block), :]
        outs[shift][:, V_AT:] = v_ref[rows(block), :]


def gather_windows(me, recv, stretch, held, out_ref, where_of):
    r = me[0]
    for u in range(N_DP):
        slot = recv[r, u]
        for c in range(N_CTX):
            where_of[stretch[c * N_DP + slot]] = u * N_CTX + c
    for shift in range(N_DP):
        slot = recv[r, replica(r, -shift)]
        for d in range(N_CTX):
            position = stretch[d * N_DP + slot]
            for m in range(BEHIND):
                source = where_of[jnp.maximum(position - BEHIND + m, 0)]
                out_ref[d, shift * BEHIND + m] = held[source]


def sum_windows(me, recv, stretch, held, out_ref, where_of):
    r = me[0]
    for shift in range(N_DP):
        slot = recv[r, replica(r, -shift)]
        for d in range(N_CTX):
            where_of[stretch[d * N_DP + slot]] = d * ENTRIES + shift * BEHIND
    for s in range(NB):
        position = stretch[s]
        total = jnp.zeros((HALF, HEAD_SIZE), jnp.float32)
        for ahead in range(1, BEHIND + 1):
            reader = position + ahead
            entry = where_of[jnp.minimum(reader, NB - 1)] + (BEHIND - ahead)
            term = held[entry].astype(jnp.float32)
            total = total + jnp.where(reader < NB, term, 0.0)
        out_ref[s] = total.astype(jnp.bfloat16)


def finish(held, own, k_out, v_out):
    for piece in range(N_CTX):
        head, half = piece // 2, piece % 2
        target = k_out if head < KEY_VALUE_HEADS else v_out
        column = (head % KEY_VALUE_HEADS) * HEAD_SIZE
        for j in range(N_DP):
            at = j * BLOCK_POSITIONS + half * HALF
            target[at : at + HALF, column : column + HEAD_SIZE] = (
                held[piece * N_DP + j].astype(jnp.float32)
                + own[at : at + HALF, head * HEAD_SIZE : (head + 1) * HEAD_SIZE]
            ).astype(jnp.bfloat16)


def dot(a, b, dims):
    return lax.dot_general(a, b, ((dims[:1], dims[1:]), ((), ())), preferred_element_type=jnp.float32)


def attend(me, recv, x0, x1, x2, x3, low_ref, win, attn, dq, sends, own):
    r = me[0]
    span = (BEHIND + 1) * BLOCK_POSITIONS
    many = GROUP * BLOCK_POSITIONS
    key_at = lax.broadcasted_iota(jnp.int32, (span, many), 0)
    query_at = lax.broadcasted_iota(jnp.int32, (span, many), 1) % BLOCK_POSITIONS + BEHIND * BLOCK_POSITIONS
    for shift, x in enumerate((x0, x1, x2, x3)):
        slot = recv[r, replica(r, -shift)]
        allowed = (key_at >= low_ref[shift : shift + 1, :]) & (key_at <= query_at)

        def head_step(h, carry, shift=shift, x=x, slot=slot, allowed=allowed):
            def window(first_piece, own_at):
                parts = [
                    win[first_piece + half, shift * BEHIND + m]
                    for m in range(BEHIND)
                    for half in range(2)
                ]
                mine = pl.ds(pl.multiple_of(own_at + h * HEAD_SIZE, HEAD_SIZE), HEAD_SIZE)
                return jnp.concatenate(parts + [x[:, mine]], axis=0)

            def stacked(base):
                parts = [
                    x[:, pl.ds(pl.multiple_of(base + h * (GROUP * HEAD_SIZE) + i * HEAD_SIZE, HEAD_SIZE), HEAD_SIZE)]
                    for i in range(GROUP)
                ]
                return jnp.concatenate(parts, axis=0)

            key = window(2 * h, K_AT)
            value = window(2 * (h + KEY_VALUE_HEADS), V_AT)
            query = stacked(0)
            grad = stacked(G_AT)
            logits = jnp.where(allowed, dot(key, query, (1, 1)) * SCALE, -1e30)
            peak = jnp.max(logits, axis=0, keepdims=True)
            weights = jnp.where(allowed, jnp.exp(logits - peak), 0.0)
            probs = weights * (1.0 / jnp.sum(weights, axis=0, keepdims=True))
            low = probs.astype(jnp.bfloat16)
            out = dot(low, value, (0, 0)).astype(jnp.bfloat16)
            dprob = dot(value, grad, (1, 1))
            delta = jnp.sum(low.astype(jnp.float32) * dprob, axis=0, keepdims=True)
            dlogit = (probs * (dprob - delta)).astype(jnp.bfloat16)
            q_grad = (dot(dlogit, key, (0, 0)) * SCALE).astype(jnp.bfloat16)
            for i in range(GROUP):
                column = pl.ds(pl.multiple_of(h * (GROUP * HEAD_SIZE) + i * HEAD_SIZE, HEAD_SIZE), HEAD_SIZE)
                part = slice(i * BLOCK_POSITIONS, (i + 1) * BLOCK_POSITIONS)
                attn[rows(slot), column] = out[part]
                dq[rows(slot), column] = q_grad[part]
            for which, term in (
                (0, dot(dlogit, query, (1, 0)) * SCALE),
                (KEY_VALUE_HEADS, dot(low, grad, (1, 0))),
            ):
                term_low = term[: BEHIND * BLOCK_POSITIONS].astype(jnp.bfloat16)
                for m in range(BEHIND):
                    for half in range(2):
                        at = m * BLOCK_POSITIONS + half * HALF
                        sends[2 * (h + which) + half, shift * BEHIND + m] = term_low[at : at + HALF]
                column = pl.ds(pl.multiple_of((h + which) * HEAD_SIZE, HEAD_SIZE), HEAD_SIZE)
                own[rows(slot), column] = term[BEHIND * BLOCK_POSITIONS :]
            return carry

        lax.fori_loop(0, KEY_VALUE_HEADS, head_step, 0)


def first_keys(stretch, docs, recv_row, me_dp, me_ctx):
    blocks = jnp.stack(
        [
            lax.dynamic_index_in_dim(
                stretch,
                me_ctx * N_DP + lax.dynamic_index_in_dim(recv_row, replica(me_dp, -shift), 0, False),
                0,
                False,
            )
            for shift in range(N_DP)
        ]
    )
    mine = jnp.take(docs.reshape(NB, BLOCK_POSITIONS), blocks, axis=0)
    start = jnp.sum((docs[None, None, :] < mine[:, :, None]).astype(jnp.int32), axis=-1)
    low = start - (blocks[:, None] - BEHIND) * BLOCK_POSITIONS
    return jnp.tile(low, (1, GROUP))


def on_device(queries, keys, values, out_grad, send_slot, recv_slot, stretch_block, doc_ids):
    me_dp = lax.axis_index("dp")
    me_ctx = lax.axis_index("ctx")
    me = me_dp.reshape(1).astype(jnp.int32)
    q, k, v, g = queries[0, 0], keys[0, 0], values[0, 0], out_grad[0, 0]
    stretch = stretch_block[0, 0]
    docs = doc_ids[0, 0]
    tokens = q.shape[0]

    kv_send = call(pack_kv, bf16(N_DP * N_CTX, HALF, HEAD_SIZE), [SMEM, SMEM, VMEM, VMEM])(
        me, send_slot, k, v
    )
    held = lax.all_to_all(kv_send, ("dp", "ctx"), 0, 0, tiled=True)
    payloads = call(
        pack_rows, [bf16(BLOCK_POSITIONS, PAYLOAD)] * N_DP, [SMEM, SMEM] + [VMEM] * 4, nbytes=9 << 19
    )(me, send_slot, q, g, k, v)
    blocks = [payloads[0]] + [
        lax.ppermute(payloads[shift], "dp", [(i, (i + shift) % N_DP) for i in range(N_DP)])
        for shift in range(1, N_DP)
    ]
    low = first_keys(
        stretch, docs, lax.dynamic_index_in_dim(recv_slot, me_dp, 0, False), me_dp, me_ctx
    )
    table = [pltpu.SMEM((NB,), jnp.int32)]
    wanted = call(
        gather_windows, bf16(N_CTX, ENTRIES, HALF, HEAD_SIZE), [SMEM] * 3 + [VMEM], table
    )(me, recv_slot, stretch, held)
    windows = lax.all_to_all(wanted, "ctx", 0, 0, tiled=True)
    attn, q_grad, sends, own = call(
        attend,
        [
            bf16(tokens, QW),
            bf16(tokens, QW),
            bf16(N_CTX, ENTRIES, HALF, HEAD_SIZE),
            jax.ShapeDtypeStruct((tokens, 2 * KW), jnp.float32),
        ],
        [SMEM, SMEM] + [VMEM] * 6,
        flops=1 << 30,
        nbytes=6 << 20,
    )(me, recv_slot, *blocks, low, windows)
    handoff = lax.ppermute(
        attn, "section", [(i, (i + 1) % lax.axis_size("section")) for i in range(lax.axis_size("section"))]
    )
    partial = lax.all_to_all(sends, "ctx", 0, 0, tiled=True)
    summed = call(
        sum_windows, bf16(NB, HALF, HEAD_SIZE), [SMEM] * 3 + [VMEM], table
    )(me, recv_slot, stretch, partial.reshape(N_CTX * ENTRIES, HALF, HEAD_SIZE))
    back = lax.all_to_all(summed.reshape(N_CTX, N_DP, HALF, HEAD_SIZE), "ctx", 0, 0, tiled=True)
    k_grad, v_grad = call(finish, [bf16(tokens, KW)] * 2, [VMEM] * 2)(
        back.reshape(NB, HALF, HEAD_SIZE), own
    )
    return handoff[None, None], q_grad[None, None], k_grad[None, None], v_grad[None, None]


def solution(mesh):
    tokens = P("dp", "section", "ctx", None)
    row = P("dp", "section", None)
    return jax.shard_map(
        on_device,
        mesh=mesh,
        in_specs=(tokens, tokens, tokens, tokens, P(), P(), row, row),
        out_specs=(tokens, tokens, tokens, tokens),
        check_vma=False,
    )
```

time: 470 us -> 175 us (0.37)
  the two profiles are of different devices: /device:TPU:2 before, /device:TPU:39 now
where the time goes in v1:
time: 175 us; the launch traced here: 174 us
  waiting for transfers between devices  73.2 us (42%)
  starting transfers between devices  38.7 us (22%)
  Pallas kernels  20.3 us (12%)
  blocking collectives  19.3 us (11%)
  local copies, waits for them, and re-layouts  12.8 us (7%)
  other arithmetic  6.55 us (4%)
  between operations  3.47 us (2%)
    all_to_all x1, waiting for transfers between devices, on_device(): partial = lax.all_to_all(sends, 'ctx', 0, 0, tiled=True)  40.5 us
    all_to_all x1, blocking collectives, on_device(): held = lax.all_to_all(kv_send, ('dp', 'ctx'), 0, 0, tiled=True)  19.3 us
    all_to_all x1, waiting for transfers between devices, on_device(): lax.all_to_all(summed.reshape(N_CTX, N_DP, HALF, HEAD_SIZE), 'ctx', 0, 0,...  15.1 us
    ppermute x3, waiting for transfers between devices, on_device(): lax.ppermute(payloads[shift], 'dp', [(i, (i + shift) % N_DP) for i in ran...  14.8 us
    pallas_call x1, Pallas kernels, on_device(): call(attend, [bf16(tokens, QW), bf16(tokens, QW), bf16(N_CTX, ENTRIES, HA...  13.2 us
    unnamed x34, local copies, waits for them, and re-layouts  10.7 us
    ppermute x1, starting transfers between devices, on_device(): lax.ppermute(attn, 'section', [(i, (i + 1) % lax.axis_size('section')) fo...  9.76 us
    ppermute x3, starting transfers between devices, on_device(): lax.ppermute(payloads[shift], 'dp', [(i, (i + shift) % N_DP) for i in ran...  8.56 us
  transfers between devices with their start and end apart: 7, of which 4 were waited for; matrix products, arithmetic and copies ran while one was open for 5% of the time, Pallas kernels for 2%

profile of v1, /device:TPU:39, one launch (start us, length us, event | category | flops | bytes accessed | tf_op | source)
XLA Modules:
  0.0 174.4 jit_solution(13979385224357045196)
XLA Ops:
  1.3 0.9 copy-done.2
  2.2 0.9 copy-done.4
  3.8 19.3 %all_to_all.20.held = bf16[64,16,128]{2,1,0:T(8,128)(2,1)S(1)} all-to-all(bf16[64,16,128]{2,1,0:T(8,128)(2,1)S(1)} %shard_map.112), channel_id=1, replica_groups=mesh['dp'=4,'ctx'=16,'section'=8] {'dp','ctx'}, dimensions={0} | all-to-all | bytes 524288 | tf_op jit(solution)/shard_map/all_to_all | solution.py:220
  23.8 1.9 %shard_map.113 = bf16[16,12,16,128]{3,2,1,0:T(8,128)(2,1)} custom-call(s32[1]{0:T(128)} %bitcast.me, s32[4,4]{1,0:T(4,128)S(1)} %copy-done.7, s32[64]{0:T(128)S(1)} %bitcast.36, bf16[64,16,128]{2,1,0:T(8,128)(2,1)S(1)} %all_to_all.20.held), custom_call_target="tpu_custom_call" | custom-call | bytes 1048576 | tf_op jit(solution)/shard_map/pallas_call | solution.py:232
  25.7 5.8 %all-to-all-start.1 = ((bf16[16,12,16,128]{3,2,1,0:T(8,128)(2,1)}), bf16[16,12,16,128]{3,2,1,0:T(8,128)(2,1)S(1)}, u32[]{:S(2)}, u32[]{:S(2)}) async-start(bf16[16,12,16,128]{3,2,1,0:T(8,128)(2,1)} %shard_map.113), calls=%async_computation.1 | async-start | bytes 1572864 | tf_op jit(solution)/shard_map/all_to_all | solution.py:235
  31.5 1.9 %shard_map.111 = (bf16[32,9216]{1,0:T(8,128)(2,1)S(1)}, bf16[32,9216]{1,0:T(8,128)(2,1)}, bf16[32,9216]{1,0:T(8,128)(2,1)}, bf16[32,9216]{1,0:T(8,128)(2,1)}) custom-call(s32[1]{0:T(128)} %bitcast.me, s32[4,4]{1,0:T(4,128)S(1)} %copy-done.8, bf16[128,4096]{1,0:T(8,128)(2,1)S(1)} %bitcast.30, bf16[128,4096]{1,0:T(8,128)(2,1)S(1)} %bitcast.31, ...), custom_call_target="tpu_custom_call" | custom-call | bytes 4718592 | tf_op jit(solution)/shard_map/pallas_call | solution.py:221
  34.2 3.8 %collective-permute-start = (bf16[32,9216]{1,0:T(8,128)(2,1)}, bf16[32,9216]{1,0:T(8,128)(2,1)S(1)}, u32[]{:S(2)}, u32[]{:S(2)}) collective-permute-start(bf16[32,9216]{1,0:T(8,128)(2,1)} %get-tuple-element.15), channel_id=1, source_target_pairs={{0,128},{128,256},{256,384},{384,0},{1,129},{129,257},{257,385},{3... | collective-permute-start | bytes 1769480 | tf_op jit(solution)/shard_map/ppermute | solution.py:225
  38.0 2.4 %collective-permute-start.1 = (bf16[32,9216]{1,0:T(8,128)(2,1)}, bf16[32,9216]{1,0:T(8,128)(2,1)S(1)}, u32[]{:S(2)}, u32[]{:S(2)}) collective-permute-start(bf16[32,9216]{1,0:T(8,128)(2,1)} %get-tuple-element.16), channel_id=1, source_target_pairs={{0,256},{128,384},{256,0},{384,128},{1,257},{129,385},{257,1},{385... | collective-permute-start | bytes 1769480 | tf_op jit(solution)/shard_map/ppermute | solution.py:225
  40.5 2.3 %collective-permute-start.2 = (bf16[32,9216]{1,0:T(8,128)(2,1)}, bf16[32,9216]{1,0:T(8,128)(2,1)S(1)}, u32[]{:S(2)}, u32[]{:S(2)}) collective-permute-start(bf16[32,9216]{1,0:T(8,128)(2,1)} %get-tuple-element.17), channel_id=1, source_target_pairs={{0,384},{128,0},{256,128},{384,256},{1,385},{129,1},{257,129},{385... | collective-permute-start | bytes 1769480 | tf_op jit(solution)/shard_map/ppermute | solution.py:225
  46.9 2.7 %fusion = s32[4]{0:T(128)S(1)} fusion(s32[1,1]{0,1:T(1,128)} %bitcast.17, s32[1,1]{0,1:T(1,128)} %bitcast.16, s32[1,1]{0,1:T(1,128)} %bitcast.15, s32[1,1]{0,1:T(1,128)} %bitcast.14), kind=kLoop, calls=%fused_computation.12 | loop fusion | flops 24 | bytes 32 | tf_op jit(solution)/shard_map/jit(_take)/jit(_where)/select_n | solution.py:202
  49.6 2.7 %add_multiply_fusion = (s32[4]{0:T(128)S(1)}, s32[4]{0:T(128)S(1)}) fusion(s32[1]{0:T(128)} %bitcast.13, s32[1]{0:T(128)} %bitcast.11, s32[1]{0:T(128)} %bitcast.9, s32[1]{0:T(128)} %bitcast.7), kind=kLoop, calls=%fused_computation.14 | loop fusion | flops 20 | bytes 48 | tf_op jit(solution)/shard_map/mul | solution.py:204
  54.7 14.8 %collective-permute-done.2.x3 = bf16[32,9216]{1,0:T(8,128)(2,1)S(1)} collective-permute-done((bf16[32,9216]{1,0:T(8,128)(2,1)}, bf16[32,9216]{1,0:T(8,128)(2,1)S(1)}, u32[]{:S(2)}, u32[]{:S(2)}) %collective-permute-start.2) | collective-permute-done | bytes 589856 | tf_op jit(solution)/shard_map/ppermute | solution.py:225
  70.3 1.1 copy-done.12
  71.4 1.1 copy-done.14
  72.5 13.2 %shard_map.114 = (bf16[128,4096]{1,0:T(8,128)(2,1)S(1)}, bf16[128,4096]{1,0:T(8,128)(2,1)}, bf16[16,12,16,128]{3,2,1,0:T(8,128)(2,1)}, f32[128,1024]{1,0:T(8,128)S(1)}) custom-call(s32[1]{0:T(128)} %bitcast.me, s32[4,4]{1,0:T(4,128)S(1)} %copy-done.7, bf16[32,9216]{1,0:T(8,128)(2,1)S(1)} %copy-done.12, bf16[32,9216]{1,0:T(8,128)(2,1)S(1)} %collective-permute-done.x1, ...), custom_call_target="tpu_custom_call" | custom-call | flops 1073741824 | bytes 6291456 | tf_op jit(solution)/shard_map/pallas_call | solution.py:236
  85.7 1.0 copy-done.9
  86.7 7.1 %all-to-all-start.2 = ((bf16[16,12,16,128]{3,2,1,0:T(8,128)(2,1)}), bf16[16,12,16,128]{3,2,1,0:T(8,128)(2,1)S(1)}, u32[]{:S(2)}, u32[]{:S(2)}) async-start(bf16[16,12,16,128]{3,2,1,0:T(8,128)(2,1)} %get-tuple-element.20), calls=%async_computation.2 | async-start | bytes 1572864 | tf_op jit(solution)/shard_map/all_to_all | solution.py:251
  93.8 9.8 %collective-permute-start.3 = (bf16[128,4096]{1,0:T(8,128)(2,1)S(1)}, bf16[128,4096]{1,0:T(8,128)(2,1)}, u32[]{:S(2)}, u32[]{:S(2)}) collective-permute-start(bf16[128,4096]{1,0:T(8,128)(2,1)S(1)} %copy-done.10), channel_id=1, source_target_pairs={{0,1},{1,2},{2,3},{3,4},{4,5},{5,6},{6,7},{7,0},{8,9},{9,10},{10,1... | collective-permute-start | bytes 3145736 | tf_op jit(solution)/shard_map/ppermute | solution.py:248
  103.5 40.5 %all-to-all-done.2 = bf16[16,12,16,128]{3,2,1,0:T(8,128)(2,1)S(1)} async-done(((bf16[16,12,16,128]{3,2,1,0:T(8,128)(2,1)}), bf16[16,12,16,128]{3,2,1,0:T(8,128)(2,1)S(1)}, u32[]{:S(2)}, u32[]{:S(2)}) %all-to-all-start.2) | async-done | bytes 786464 | tf_op jit(solution)/shard_map/all_to_all | solution.py:251
  144.1 1.9 %shard_map.115 = bf16[64,16,128]{2,1,0:T(8,128)(2,1)} custom-call(s32[1]{0:T(128)} %bitcast.me, s32[4,4]{1,0:T(4,128)S(1)} %copy-done.7, s32[64]{0:T(128)S(1)} %bitcast.37, bf16[192,16,128]{2,1,0:T(8,128)(2,1)S(1)} %bitcast.28), custom_call_target="tpu_custom_call" | custom-call | bytes 1048576 | tf_op jit(solution)/shard_map/pallas_call | solution.py:252
  145.9 7.6 %all-to-all-start.3 = ((bf16[16,4,16,128]{3,2,1,0:T(8,128)(2,1)}), bf16[16,4,16,128]{3,2,1,0:T(8,128)(2,1)S(1)}, u32[]{:S(2)}, u32[]{:S(2)}) async-start(bf16[16,4,16,128]{3,2,1,0:T(8,128)(2,1)} %bitcast.23), calls=%async_computation.3 | async-start | bytes 524288 | tf_op jit(solution)/shard_map/all_to_all | solution.py:255
  153.5 2.8 %collective-permute-done.3 = bf16[128,4096]{1,0:T(8,128)(2,1)} collective-permute-done((bf16[128,4096]{1,0:T(8,128)(2,1)S(1)}, bf16[128,4096]{1,0:T(8,128)(2,1)}, u32[]{:S(2)}, u32[]{:S(2)}) %collective-permute-start.3) | collective-permute-done | bytes 1048608 | tf_op jit(solution)/shard_map/ppermute | solution.py:248
  156.3 15.1 %all-to-all-done.3 = bf16[16,4,16,128]{3,2,1,0:T(8,128)(2,1)S(1)} async-done(((bf16[16,4,16,128]{3,2,1,0:T(8,128)(2,1)}), bf16[16,4,16,128]{3,2,1,0:T(8,128)(2,1)S(1)}, u32[]{:S(2)}, u32[]{:S(2)}) %all-to-all-start.3) | async-done | bytes 262176 | tf_op jit(solution)/shard_map/all_to_all | solution.py:255
  172.1 2.3 %copy.13 = bf16[1,1,128,4096]{3,2,1,0:T(8,128)(2,1)} copy(bf16[1,1,128,4096]{3,2,1,0:T(8,128)(2,1)} %bitcast.20) | data formatting | bytes 2097152
  (45 shorter events, 8.1 us)
Async XLA Ops:
  0.6 0.7 copy-start.8
  1.3 0.9 copy-start.2
  2.2 0.9 copy-start.4
  3.8 19.4 %copy-start.7 = (s32[4,4]{1,0:T(4,128)S(1)}, s32[4,4]{1,0:T(4,128)}, u32[]{:S(2)}) copy-start(s32[4,4]{1,0:T(4,128)} %recv.5) | copy-start | bytes 196
  23.1 0.7 copy-start.6
  23.8 7.7 %copy-start.1 = (bf16[1,1,128,4096]{3,2,1,0:T(8,128)(2,1)S(1)}, bf16[1,1,128,4096]{3,2,1,0:T(8,128)(2,1)}, u32[]{:S(2)}) copy-start(bf16[1,1,128,4096]{3,2,1,0:T(8,128)(2,1)} %param.11) | copy-start | bytes 3145732
  25.7 5.8 %copy-start = (bf16[1,1,128,4096]{3,2,1,0:T(8,128)(2,1)S(1)}, bf16[1,1,128,4096]{3,2,1,0:T(8,128)(2,1)}, u32[]{:S(2)}) copy-start(bf16[1,1,128,4096]{3,2,1,0:T(8,128)(2,1)} %param.8) | copy-start | bytes 3145732
  25.7 5.8 %copy-start.3 = (bf16[1,1,128,512]{3,2,1,0:T(8,128)(2,1)S(1)}, bf16[1,1,128,512]{3,2,1,0:T(8,128)(2,1)}, u32[]{:S(2)}) copy-start(bf16[1,1,128,512]{3,2,1,0:T(8,128)(2,1)} %param.9) | copy-start | bytes 393220
  25.7 5.8 %copy-start.5 = (bf16[1,1,128,512]{3,2,1,0:T(8,128)(2,1)S(1)}, bf16[1,1,128,512]{3,2,1,0:T(8,128)(2,1)}, u32[]{:S(2)}) copy-start(bf16[1,1,128,512]{3,2,1,0:T(8,128)(2,1)} %param.10) | copy-start | bytes 393220
  25.7 44.6 %all-to-all-start.1 = ((bf16[16,12,16,128]{3,2,1,0:T(8,128)(2,1)}), bf16[16,12,16,128]{3,2,1,0:T(8,128)(2,1)S(1)}, u32[]{:S(2)}, u32[]{:S(2)}) async-start(bf16[16,12,16,128]{3,2,1,0:T(8,128)(2,1)} %shard_map.113), calls=%async_computation.1 | async-start | bytes 1572864 | tf_op jit(solution)/shard_map/all_to_all | solution.py:235
  33.4 0.8 copy-start.11
  34.2 20.4 %collective-permute-start = (bf16[32,9216]{1,0:T(8,128)(2,1)}, bf16[32,9216]{1,0:T(8,128)(2,1)S(1)}, u32[]{:S(2)}, u32[]{:S(2)}) collective-permute-start(bf16[32,9216]{1,0:T(8,128)(2,1)} %get-tuple-element.15), channel_id=1, source_target_pairs={{0,128},{128,256},{256,384},{384,0},{1,129},{129,257},{257,385},{3... | collective-permute-start | bytes 1769480 | tf_op jit(solution)/shard_map/ppermute | solution.py:225
  38.0 16.7 %collective-permute-start.1 = (bf16[32,9216]{1,0:T(8,128)(2,1)}, bf16[32,9216]{1,0:T(8,128)(2,1)S(1)}, u32[]{:S(2)}, u32[]{:S(2)}) collective-permute-start(bf16[32,9216]{1,0:T(8,128)(2,1)} %get-tuple-element.16), channel_id=1, source_target_pairs={{0,256},{128,384},{256,0},{384,128},{1,257},{129,385},{257,1},{385... | collective-permute-start | bytes 1769480 | tf_op jit(solution)/shard_map/ppermute | solution.py:225
  40.5 29.0 %collective-permute-start.2 = (bf16[32,9216]{1,0:T(8,128)(2,1)}, bf16[32,9216]{1,0:T(8,128)(2,1)S(1)}, u32[]{:S(2)}, u32[]{:S(2)}) collective-permute-start(bf16[32,9216]{1,0:T(8,128)(2,1)} %get-tuple-element.17), channel_id=1, source_target_pairs={{0,384},{128,0},{256,128},{384,256},{1,385},{129,1},{257,129},{385... | collective-permute-start | bytes 1769480 | tf_op jit(solution)/shard_map/ppermute | solution.py:225
  49.6 3.3 %copy-start.15 = (s32[1,1,2048]{2,1,0:T(1,128)S(1)}, s32[1,1,2048]{2,1,0:T(1,128)}, u32[]{:S(2)}) copy-start(s32[1,1,2048]{2,1,0:T(1,128)} %param.15) | copy-start | bytes 24580
  69.5 0.8 copy-start.13
  70.3 1.1 copy-start.12
  71.4 1.1 copy-start.14
  85.7 1.0 copy-start.9
  86.7 7.1 %copy-start.10 = (bf16[128,4096]{1,0:T(8,128)(2,1)S(1)}, bf16[128,4096]{1,0:T(8,128)(2,1)}, u32[]{:S(2)}) copy-start(bf16[128,4096]{1,0:T(8,128)(2,1)} %copy-done.9) | copy-start | bytes 3145732
  86.7 57.4 %all-to-all-start.2 = ((bf16[16,12,16,128]{3,2,1,0:T(8,128)(2,1)}), bf16[16,12,16,128]{3,2,1,0:T(8,128)(2,1)S(1)}, u32[]{:S(2)}, u32[]{:S(2)}) async-start(bf16[16,12,16,128]{3,2,1,0:T(8,128)(2,1)} %get-tuple-element.20), calls=%async_computation.2 | async-start | bytes 1572864 | tf_op jit(solution)/shard_map/all_to_all | solution.py:251
  93.8 62.5 %collective-permute-start.3 = (bf16[128,4096]{1,0:T(8,128)(2,1)S(1)}, bf16[128,4096]{1,0:T(8,128)(2,1)}, u32[]{:S(2)}, u32[]{:S(2)}) collective-permute-start(bf16[128,4096]{1,0:T(8,128)(2,1)S(1)} %copy-done.10), channel_id=1, source_target_pairs={{0,1},{1,2},{2,3},{3,4},{4,5},{5,6},{6,7},{7,0},{8,9},{9,10},{10,1... | collective-permute-start | bytes 3145736 | tf_op jit(solution)/shard_map/ppermute | solution.py:248
  145.9 25.5 %all-to-all-start.3 = ((bf16[16,4,16,128]{3,2,1,0:T(8,128)(2,1)}), bf16[16,4,16,128]{3,2,1,0:T(8,128)(2,1)S(1)}, u32[]{:S(2)}, u32[]{:S(2)}) async-start(bf16[16,4,16,128]{3,2,1,0:T(8,128)(2,1)} %bitcast.23), calls=%async_computation.3 | async-start | bytes 524288 | tf_op jit(solution)/shard_map/all_to_all | solution.py:255

commit v2 on v1

v2 whole, which is shorter than its diff:
```python
import math

import jax
import jax.numpy as jnp
from jax import lax
from jax.experimental import pallas as pl
from jax.experimental.pallas import tpu as pltpu
from jax.sharding import PartitionSpec as P

QUERY_HEADS = 32
KEY_VALUE_HEADS = 4
HEAD_SIZE = 128
BLOCK_POSITIONS = 32
N_DP = 4
N_CTX = 16
NB = 64
GROUP = QUERY_HEADS // KEY_VALUE_HEADS
QW = QUERY_HEADS * HEAD_SIZE
KW = KEY_VALUE_HEADS * HEAD_SIZE
K_AT = QW
V_AT = QW + KW
G_AT = QW + 2 * KW
PAYLOAD = 2 * QW + 2 * KW
PIECES = 2 * KEY_VALUE_HEADS
BEHIND = 3
ENTRIES = N_DP * BEHIND
SCALE = HEAD_SIZE ** (-0.5)
LOG2_E = math.log2(math.e)
SPAN = (BEHIND + 1) * BLOCK_POSITIONS

VMEM = pl.BlockSpec(memory_space=pltpu.VMEM)
SMEM = pl.BlockSpec(memory_space=pltpu.SMEM)
ANY = pl.BlockSpec(memory_space=pl.ANY)
HBM = pl.BlockSpec(memory_space=pltpu.HBM)


def call(
    kernel, out_shape, in_specs, scratch=(), flops=0, nbytes=1 << 20, out_space=VMEM, aliases={}, limit=40
):
    if isinstance(out_shape, list) and not isinstance(out_space, list):
        out_space = [out_space] * len(out_shape)
    return pl.pallas_call(
        kernel,
        out_shape=out_shape,
        in_specs=in_specs,
        out_specs=out_space,
        scratch_shapes=scratch,
        input_output_aliases=aliases,
        compiler_params=pltpu.CompilerParams(vmem_limit_bytes=limit << 20),
        cost_estimate=pl.CostEstimate(flops=flops, bytes_accessed=nbytes, transcendentals=0),
    )


def bf16(*shape):
    return jax.ShapeDtypeStruct(shape, jnp.bfloat16)


def replica(me, shift):
    return lax.rem(me + shift + N_DP, N_DP)


def rows(block):
    return pl.ds(pl.multiple_of(block * BLOCK_POSITIONS, BLOCK_POSITIONS), BLOCK_POSITIONS)


def pack(me, send, q_ref, g_ref, k_ref, v_ref, pieces, own, plus, minus, far, far_g, k_rows, v_rows, sems):
    r = me[0]
    copies = [
        pltpu.make_async_copy(k_ref, k_rows, sems.at[0]),
        pltpu.make_async_copy(v_ref, v_rows, sems.at[1]),
    ]
    for shift, main, grad in ((1, plus, plus), (3, minus, minus), (2, far, far_g), (0, own, own)):
        source = rows(send[r, replica(r, shift)])
        for ref, target, column in ((q_ref, main, 0), (g_ref, grad, 0 if shift == 2 else G_AT)):
            copies.append(
                pltpu.make_async_copy(
                    ref.at[source], target.at[:, column : column + QW], sems.at[len(copies)]
                )
            )
    for copy in copies:
        copy.start()
    copies[0].wait()
    copies[1].wait()
    for u in range(N_DP):
        block = send[r, u]
        for piece in range(PIECES):
            source = k_rows if piece < KEY_VALUE_HEADS else v_rows
            column = (piece % KEY_VALUE_HEADS) * HEAD_SIZE
            part = source[rows(block), column : column + HEAD_SIZE]
            for c in range(piece, N_CTX, PIECES):
                pieces[u * N_CTX + c] = part
    for shift, target in ((1, plus), (3, minus), (2, far), (0, own)):
        block = send[r, replica(r, shift)]
        target[:, K_AT:V_AT] = k_rows[rows(block), :]
        target[:, V_AT:G_AT] = v_rows[rows(block), :]
    for copy in copies[2:]:
        copy.wait()


def gather_windows(me, recv, stretch, held, plus, minus, docs, out_ref, where_of):
    r = me[0]
    first = (me[1] // PIECES) * PIECES
    for u in range(N_DP):
        slot = recv[r, u]
        for c in range(N_CTX):
            where_of[stretch[c * N_DP + slot]] = u * N_CTX + c
    for shift in range(N_DP):
        slot = recv[r, replica(r, -shift)]
        for d in range(PIECES):
            position = stretch[(first + d) * N_DP + slot]
            for m in range(BEHIND):
                source = where_of[jnp.maximum(position - BEHIND + m, 0)]
                out_ref[d, shift * BEHIND + m] = held[source]


def sum_windows(me, recv, stretch, held, handoff, out_ref, where_of):
    r = me[0]
    first = (me[1] // PIECES) * PIECES
    for position in range(NB):
        where_of[position] = -1
    for shift in range(N_DP):
        slot = recv[r, replica(r, -shift)]
        for d in range(PIECES):
            where_of[stretch[(first + d) * N_DP + slot]] = d * ENTRIES + shift * BEHIND
    for s in range(NB):
        position = stretch[s]
        total = jnp.zeros((BLOCK_POSITIONS, HEAD_SIZE), jnp.float32)
        for ahead in range(1, BEHIND + 1):
            reader = position + ahead
            entry = where_of[jnp.minimum(reader, NB - 1)]
            here = (reader < NB) & (entry >= 0)
            term = held[jnp.maximum(entry, 0) + (BEHIND - ahead)].astype(jnp.float32)
            total = total + jnp.where(here, term, 0.0)
        out_ref[s] = total.astype(jnp.bfloat16)


def finish(held, own, k_out, v_out):
    for piece in range(PIECES):
        target = k_out if piece < KEY_VALUE_HEADS else v_out
        column = (piece % KEY_VALUE_HEADS) * HEAD_SIZE
        for j in range(N_DP):
            at = slice(j * BLOCK_POSITIONS, (j + 1) * BLOCK_POSITIONS)
            total = own[at, piece * HEAD_SIZE : (piece + 1) * HEAD_SIZE]
            for c in range(piece, N_CTX, PIECES):
                total = total + held[c * N_DP + j].astype(jnp.float32)
            target[at, column : column + HEAD_SIZE] = total.astype(jnp.bfloat16)


def dot(a, b, dims):
    return lax.dot_general(a, b, ((dims[:1], dims[1:]), ((), ())), preferred_element_type=jnp.float32)


def window_of(win, x, shift, head, own_at):
    parts = [win[head, shift * BEHIND + m] for m in range(BEHIND)]
    return jnp.concatenate(parts + [x[:, own_at : own_at + HEAD_SIZE]], axis=0)


def stacked(x, base, head):
    at = base + head * GROUP * HEAD_SIZE
    parts = [x[:, at + i * HEAD_SIZE : at + (i + 1) * HEAD_SIZE] for i in range(GROUP)]
    return jnp.concatenate(parts, axis=0)


def unstack(target, slot, head, tall):
    for i in range(GROUP):
        at = (head * GROUP + i) * HEAD_SIZE
        target[rows(slot), at : at + HEAD_SIZE] = tall[i * BLOCK_POSITIONS : (i + 1) * BLOCK_POSITIONS]


def forward(me, recv, stretch, own_block, plus, far, minus, docs, win, *outs):
    r = me[0]
    key_at = lax.broadcasted_iota(jnp.int32, (SPAN, SPAN), 0)
    query_at = lax.broadcasted_iota(jnp.int32, (SPAN, SPAN), 1) % BLOCK_POSITIONS
    causal = key_at <= query_at + BEHIND * BLOCK_POSITIONS
    for shift, x in enumerate((own_block, plus, far, minus)):
        slot = recv[r, replica(r, -shift)]
        row = docs[pl.ds(stretch[me[1] * N_DP + slot], 1), :]
        key_doc = jnp.transpose(jnp.broadcast_to(row, (SPAN, SPAN)))
        query_doc = jnp.tile(row[:, BEHIND * BLOCK_POSITIONS :], (1, SPAN // BLOCK_POSITIONS))
        bias = jnp.where((key_doc == query_doc) & causal, 0.0, -1e30)
        bias = jnp.concatenate([bias, bias], axis=1)
        for head in range(KEY_VALUE_HEADS):
            key = window_of(win, x, shift, head, K_AT + head * HEAD_SIZE)
            value = window_of(win, x, shift, head + KEY_VALUE_HEADS, V_AT + head * HEAD_SIZE)
            logits = dot(key, stacked(x, 0, head), (1, 1)) * (SCALE * LOG2_E) + bias
            weights = jnp.exp2(logits - jnp.max(logits, axis=0, keepdims=True))
            probs = weights * (1.0 / jnp.sum(weights, axis=0, keepdims=True))
            outs[-1][shift * KEY_VALUE_HEADS + head] = probs
            out = dot(probs.astype(jnp.bfloat16), value, (0, 0)).astype(jnp.bfloat16)
            unstack(outs[0], slot, head, out)


def backward(me, recv, own_block, plus, far, minus, far_g, win, probs_in, dq, sends, own):
    r = me[0]
    for shift, x in enumerate((own_block, plus, far, minus)):
        slot = recv[r, replica(r, -shift)]
        for head in range(KEY_VALUE_HEADS):
            key = window_of(win, x, shift, head, K_AT + head * HEAD_SIZE)
            value = window_of(win, x, shift, head + KEY_VALUE_HEADS, V_AT + head * HEAD_SIZE)
            query = stacked(x, 0, head)
            grad = stacked(far_g, 0, head) if shift == 2 else stacked(x, G_AT, head)
            probs = probs_in[shift * KEY_VALUE_HEADS + head]
            low = probs.astype(jnp.bfloat16)
            dprob = dot(value, grad, (1, 1))
            delta = jnp.sum(low.astype(jnp.float32) * dprob, axis=0, keepdims=True)
            dlogit = (probs * (dprob - delta)).astype(jnp.bfloat16)
            unstack(dq, slot, head, (dot(dlogit, key, (0, 0)) * SCALE).astype(jnp.bfloat16))
            for column, term in (
                (head, dot(dlogit, query, (1, 0)) * SCALE),
                (head + KEY_VALUE_HEADS, dot(low, grad, (1, 0))),
            ):
                term_low = term[: BEHIND * BLOCK_POSITIONS].astype(jnp.bfloat16)
                for m in range(BEHIND):
                    sends[column, shift * BEHIND + m] = term_low[m * BLOCK_POSITIONS : (m + 1) * BLOCK_POSITIONS]
                own[rows(slot), column * HEAD_SIZE : (column + 1) * HEAD_SIZE] = term[BEHIND * BLOCK_POSITIONS :]


def window_docs(docs):
    padded = jnp.concatenate([jnp.full((BEHIND * BLOCK_POSITIONS,), -1, jnp.int32), docs])
    padded = padded.reshape(NB + BEHIND, BLOCK_POSITIONS)
    return jnp.concatenate([padded[m : m + NB] for m in range(BEHIND + 1)], axis=1)


def on_device(queries, keys, values, out_grad, send_slot, recv_slot, stretch_block, doc_ids):
    me = jnp.stack([lax.axis_index("dp"), lax.axis_index("ctx")]).astype(jnp.int32)
    q, k, v, g = queries[0, 0], keys[0, 0], values[0, 0], out_grad[0, 0]
    stretch = stretch_block[0, 0]
    tokens = q.shape[0]
    n_section = lax.axis_size("section")

    pieces, own_block, plus, minus, far, far_g = call(
        pack,
        [bf16(N_DP * N_CTX, BLOCK_POSITIONS, HEAD_SIZE)]
        + [bf16(BLOCK_POSITIONS, width) for width in (PAYLOAD, PAYLOAD, PAYLOAD, G_AT, QW)],
        [SMEM, SMEM] + [ANY] * 4,
        [pltpu.VMEM((tokens, KW), jnp.bfloat16)] * 2 + [pltpu.SemaphoreType.DMA((2 + 2 * N_DP,))],
        nbytes=9 << 19,
    )(me, send_slot, *(pltpu.with_memory_space_constraint(x, pltpu.HBM) for x in (q, g, k, v)))
    held = lax.all_to_all(pieces, ("dp", "ctx"), 0, 0, tiled=True)
    ahead = [(i, (i + 1) % N_DP) for i in range(N_DP)]
    behind = [(i, (i - 1) % N_DP) for i in range(N_DP)]
    plus = lax.ppermute(plus, "dp", ahead)
    minus = lax.ppermute(minus, "dp", behind)
    far = lax.ppermute(far, "dp", [(i, (i + 2) % N_DP) for i in range(N_DP)])
    far_g = lax.ppermute(far_g, "dp", [(i, (i + 2) % N_DP) for i in range(N_DP)])
    docs = window_docs(doc_ids[0, 0])
    table = [pltpu.SMEM((NB,), jnp.int32)]
    wanted = call(
        gather_windows, bf16(PIECES, ENTRIES, BLOCK_POSITIONS, HEAD_SIZE), [SMEM] * 3 + [VMEM] + [ANY] * 3, table
    )(me, recv_slot, stretch, held, plus, minus, docs)
    halves = [list(range(at, at + PIECES)) for at in range(0, N_CTX, PIECES)]
    windows = lax.all_to_all(wanted, "ctx", 0, 0, tiled=True, axis_index_groups=halves)
    attn, probs = call(
        forward,
        [bf16(tokens, QW), jax.ShapeDtypeStruct((N_DP * KEY_VALUE_HEADS, SPAN, GROUP * BLOCK_POSITIONS), jnp.float32)],
        [SMEM] * 3 + [VMEM] * 6,
        flops=1 << 29,
        nbytes=6 << 20,
    )(me, recv_slot, stretch, own_block, plus, far, minus, docs, windows)
    onward = [(i, (i + 1) % n_section) for i in range(n_section)]
    odd = lax.axis_index("section") % 2 == 1
    hop = lax.ppermute(attn, "section", [(i, (i + 2) % n_section) for i in range(1, n_section, 2)])
    handoff = lax.ppermute(jnp.where(odd, hop, attn), "section", [(i, i ^ 1) for i in range(n_section)])
    q_grad, sends, own = call(
        backward,
        [
            bf16(tokens, QW),
            bf16(PIECES, ENTRIES, BLOCK_POSITIONS, HEAD_SIZE),
            jax.ShapeDtypeStruct((tokens, 2 * KW), jnp.float32),
        ],
        [SMEM] * 2 + [VMEM] * 7,
        flops=1 << 30,
        nbytes=6 << 20,
    )(me, recv_slot, own_block, plus, far, minus, far_g, windows, probs)
    partial = lax.all_to_all(sends, "ctx", 0, 0, tiled=True, axis_index_groups=halves)
    summed = call(
        sum_windows,
        bf16(NB, BLOCK_POSITIONS, HEAD_SIZE),
        [SMEM] * 3 + [VMEM] + [ANY],
        table,
    )(me, recv_slot, stretch, partial.reshape(PIECES * ENTRIES, BLOCK_POSITIONS, HEAD_SIZE), handoff)
    back = lax.all_to_all(summed.reshape(N_CTX, N_DP, BLOCK_POSITIONS, HEAD_SIZE), "ctx", 0, 0, tiled=True)
    k_grad, v_grad = call(finish, [bf16(tokens, KW)] * 2, [VMEM] * 2)(
        back.reshape(NB, BLOCK_POSITIONS, HEAD_SIZE), own
    )
    return handoff[None, None], q_grad[None, None], k_grad[None, None], v_grad[None, None]


def solution(mesh):
    tokens = P("dp", "section", "ctx", None)
    row = P("dp", "section", None)
    return jax.shard_map(
        on_device,
        mesh=mesh,
        in_specs=(tokens, tokens, tokens, tokens, P(), P(), row, row),
        out_specs=(tokens, tokens, tokens, tokens),
        check_vma=False,
    )
```

time: 175 us -> 151 us (0.86)
  the two profiles are of different devices: /device:TPU:39 before, /device:TPU:2 now
where the time goes in v2:
time: 151 us; the launch traced here: 150 us
  waiting for transfers between devices  73.4 us (49%)
  starting transfers between devices  52.8 us (35%)
  Pallas kernels  16.1 us (11%)
  local copies, waits for them, and re-layouts  5.09 us (3%)
  other arithmetic  2.2 us (1%)
    all_to_all x1, waiting for transfers between devices, on_device(): lax.all_to_all(sends, 'ctx', 0, 0, tiled=True, axis_index_groups=halves)  33.9 us
    all_to_all x1, waiting for transfers between devices, on_device(): lax.all_to_all(summed.reshape(N_CTX, N_DP, BLOCK_POSITIONS, HEAD_SIZE), '...  15.8 us
    all_to_all x1, starting transfers between devices, on_device(): held = lax.all_to_all(pieces, ('dp', 'ctx'), 0, 0, tiled=True)  12.1 us
    ppermute x1, waiting for transfers between devices, on_device(): plus = lax.ppermute(plus, 'dp', ahead)  11.9 us
    all_to_all x1, starting transfers between devices, on_device(): lax.all_to_all(summed.reshape(N_CTX, N_DP, BLOCK_POSITIONS, HEAD_SIZE), '...  9.8 us
    ppermute x1, waiting for transfers between devices, on_device(): far = lax.ppermute(far, 'dp', [(i, (i + 2) % N_DP) for i in range(N_DP)])  6.89 us
    all_to_all x1, starting transfers between devices, on_device(): lax.all_to_all(sends, 'ctx', 0, 0, tiled=True, axis_index_groups=halves)  5.7 us
    ppermute x1, starting transfers between devices, on_device(): lax.ppermute(jnp.where(odd, hop, attn), 'section', [(i, i ^ 1) for i in r...  5.35 us
  transfers between devices with their start and end apart: 10, of which 6 were waited for; matrix products, arithmetic and copies ran while one was open for 2% of the time, Pallas kernels for 5%

profile of v2, /device:TPU:2, one launch (start us, length us, event | category | flops | bytes accessed | tf_op | source)
XLA Modules:
  0.0 150.4 jit_solution(7341411124924129112)
XLA Ops:
  1.4 3.4 %shard_map.111 = (bf16[64,32,128]{2,1,0:T(8,128)(2,1)}, bf16[32,9216]{1,0:T(8,128)(2,1)S(1)}, bf16[32,9216]{1,0:T(8,128)(2,1)}, bf16[32,9216]{1,0:T(8,128)(2,1)S...) custom-call(s32[2]{0:T(128)S(1)} %pad_add_fusion.1.me, s32[4,4]{1,0:T(4,128)S(1)} %copy-done.5, ...), custom_call_target="tpu_custom_call" | custom-call | bytes 4718592 | tf_op jit(solution)/shard_map/pallas_call | solution.py:231
  4.8 12.1 %all-to-all-start = ((bf16[64,32,128]{2,1,0:T(8,128)(2,1)}), bf16[64,32,128]{2,1,0:T(8,128)(2,1)S(1)}, u32[]{:S(2)}, u32[]{:S(2)}) async-start(bf16[64,32,128]{2,1,0:T(8,128)(2,1)} %get-tuple-element.21), calls=%async_computation | async-start | bytes 1048576 | tf_op jit(solution)/shard_map/all_to_all | solution.py:239
  16.9 3.5 %collective-permute-start = (bf16[32,9216]{1,0:T(8,128)(2,1)}, bf16[32,9216]{1,0:T(8,128)(2,1)S(1)}, u32[]{:S(2)}, u32[]{:S(2)}) collective-permute-start(bf16[32,9216]{1,0:T(8,128)(2,1)} %get-tuple-element.18), channel_id=1, source_target_pairs={{0,128},{128,256},{256,384},{384,0},{1,129},{129,257},{257,385},{3... | collective-permute-start | bytes 1769480 | tf_op jit(solution)/shard_map/ppermute | solution.py:242
  20.4 2.4 %collective-permute-start.2 = (bf16[32,9216]{1,0:T(8,128)(2,1)S(1)}, bf16[32,9216]{1,0:T(8,128)(2,1)S(1)}, u32[]{:S(2)}, u32[]{:S(2)}) collective-permute-start(bf16[32,9216]{1,0:T(8,128)(2,1)S(1)} %get-tuple-element.20), channel_id=1, source_target_pairs={{0,384},{128,0},{256,128},{384,256},{1,385},{129,1},{257,129},{385... | collective-permute-start | bytes 1769480 | tf_op jit(solution)/shard_map/ppermute | solution.py:243
  24.5 11.9 %collective-permute-done.plus = bf16[32,9216]{1,0:T(8,128)(2,1)S(1)} collective-permute-done((bf16[32,9216]{1,0:T(8,128)(2,1)}, bf16[32,9216]{1,0:T(8,128)(2,1)S(1)}, u32[]{:S(2)}, u32[]{:S(2)}) %collective-permute-start) | collective-permute-done | bytes 589856 | tf_op jit(solution)/shard_map/ppermute | solution.py:242
  36.4 2.6 %collective-permute-done.2.minus = bf16[32,9216]{1,0:T(8,128)(2,1)S(1)} collective-permute-done((bf16[32,9216]{1,0:T(8,128)(2,1)S(1)}, bf16[32,9216]{1,0:T(8,128)(2,1)S(1)}, u32[]{:S(2)}, u32[]{:S(2)}) %collective-permute-start.2) | collective-permute-done | bytes 589856 | tf_op jit(solution)/shard_map/ppermute | solution.py:243
  39.0 1.8 %shard_map.112 = bf16[8,12,32,128]{3,2,1,0:T(8,128)(2,1)} custom-call(s32[2]{0:T(128)S(1)} %pad_add_fusion.1.me, s32[4,4]{1,0:T(4,128)S(1)} %copy-done.3, s32[64]{0:T(128)S(1)} %bitcast.18, bf16[64,32,128]{2,1,0:T(8,128)(2,1)S(1)} %all-to-all-done.held, bf16[32,9216]{1,0:T(8,128)(2,1)S(1)} %collective-permute-done.plus, ...), custom_call_target="tpu_custom_call" | custom-call | bytes 1048576 | tf_op jit(solution)/shard_map/pallas_call | solution.py:248
  40.7 5.1 %all-to-all-start.1 = ((bf16[8,12,32,128]{3,2,1,0:T(8,128)(2,1)}), bf16[8,12,32,128]{3,2,1,0:T(8,128)(2,1)S(1)}, u32[]{:S(2)}, u32[]{:S(2)}) async-start(bf16[8,12,32,128]{3,2,1,0:T(8,128)(2,1)} %shard_map.112), calls=%async_computation.1 | async-start | bytes 1572864 | tf_op jit(solution)/shard_map/all_to_all | solution.py:252
  45.8 3.6 %collective-permute-start.1 = (bf16[32,5120]{1,0:T(8,128)(2,1)}, bf16[32,5120]{1,0:T(8,128)(2,1)S(1)}, u32[]{:S(2)}, u32[]{:S(2)}) collective-permute-start(bf16[32,5120]{1,0:T(8,128)(2,1)} %get-tuple-element.19), channel_id=1, source_target_pairs={{0,256},{128,384},{256,0},{384,128},{1,257},{129,385},{257,1},{385... | collective-permute-start | bytes 983048 | tf_op jit(solution)/shard_map/ppermute | solution.py:244
  49.4 3.8 %collective-permute-start.5 = (bf16[32,4096]{1,0:T(8,128)(2,1)}, bf16[32,4096]{1,0:T(8,128)(2,1)S(1)}, u32[]{:S(2)}, u32[]{:S(2)}) collective-permute-start(bf16[32,4096]{1,0:T(8,128)(2,1)} %copy-done.6), channel_id=1, source_target_pairs={{0,256},{128,384},{256,0},{384,128},{1,257},{129,385},{257,1},{385... | collective-permute-start | bytes 786440 | tf_op jit(solution)/shard_map/ppermute | solution.py:245
  53.2 6.9 %collective-permute-done.1.far = bf16[32,5120]{1,0:T(8,128)(2,1)S(1)} collective-permute-done((bf16[32,5120]{1,0:T(8,128)(2,1)}, bf16[32,5120]{1,0:T(8,128)(2,1)S(1)}, u32[]{:S(2)}, u32[]{:S(2)}) %collective-permute-start.1) | collective-permute-done | bytes 327712 | tf_op jit(solution)/shard_map/ppermute | solution.py:244
  60.1 3.1 %shard_map.113 = (bf16[128,4096]{1,0:T(8,128)(2,1)}, f32[16,128,256]{2,1,0:T(8,128)S(1)}) custom-call(s32[2]{0:T(128)S(1)} %pad_add_fusion.1.me, s32[4,4]{1,0:T(4,128)S(1)} %copy-done.3, s32[64]{0:T(128)S(1)} %bitcast.19, bf16[32,9216]{1,0:T(8,128)(2,1)S(1)} %get-tuple-element.17.own_block, bf16[32,9216]{1,0:T(8,128)(2,1)S(1)} %collective-permute-done.plus, ...), custom_call_target="tpu_custom_call" | custom-call | flops 536870912 | bytes 6291456 | tf_op jit(solution)/shard_map/pallas_call | solution.py:253
  63.1 1.6 %collective-permute-start.3 = (bf16[128,4096]{1,0:T(8,128)(2,1)}, bf16[128,4096]{1,0:T(8,128)(2,1)}, u32[]{:S(2)}, u32[]{:S(2)}) collective-permute-start(bf16[128,4096]{1,0:T(8,128)(2,1)} %get-tuple-element.22), channel_id=1, source_target_pairs={{1,3},{3,5},{5,7},{7,1},{9,11},{11,13},{13,15},{15,9},{17,19},{19,... | collective-permute-start | bytes 3145736 | tf_op jit(solution)/shard_map/ppermute | solution.py:262
  65.5 0.9 copy-done.2
  66.4 5.0 %shard_map.114 = (bf16[128,4096]{1,0:T(8,128)(2,1)}, bf16[8,12,32,128]{3,2,1,0:T(8,128)(2,1)S(1)}, f32[128,1024]{1,0:T(8,128)S(1)}) custom-call(s32[2]{0:T(128)S(1)} %pad_add_fusion.1.me, s32[4,4]{1,0:T(4,128)S(1)} %copy-done.3, bf16[32,9216]{1,0:T(8,128)(2,1)S(1)} %get-tuple-element.17.own_block, bf16[32,9216]{1,0:T(8,128)(2,1)S(1)} %collective-permute-done.plus, ...), custom_call_target="tpu_custom_call" | custom-call | flops 1073741824 | bytes 6291456 | tf_op jit(solution)/shard_map/pallas_call | solution.py:264
  72.3 5.7 %all-to-all-start.2 = ((bf16[8,12,32,128]{3,2,1,0:T(8,128)(2,1)}), bf16[8,12,32,128]{3,2,1,0:T(8,128)(2,1)S(1)}, u32[]{:S(2)}, u32[]{:S(2)}) async-start(bf16[8,12,32,128]{3,2,1,0:T(8,128)(2,1)} %copy-done), calls=%async_computation.2 | async-start | bytes 1572864 | tf_op jit(solution)/shard_map/all_to_all | solution.py:275
  78.0 1.3 broadcast_select_fusion
  79.3 5.3 %collective-permute-start.4 = (bf16[128,4096]{1,0:T(8,128)(2,1)S(1)}, bf16[128,4096]{1,0:T(8,128)(2,1)S(1)}, u32[]{:S(2)}, u32[]{:S(2)}) collective-permute-start(bf16[128,4096]{1,0:T(8,128)(2,1)S(1)} %broadcast_select_fusion), channel_id=1, source_target_pairs={{0,1},{1,0},{2,3},{3,2},{4,5},{5,4},{6,7},{7,6},{8,9},{9,8},{10,11... | collective-permute-start | bytes 3145736 | tf_op jit(solution)/shard_map/ppermute | solution.py:263
  84.7 2.3 %collective-permute-done.4.handoff = bf16[128,4096]{1,0:T(8,128)(2,1)S(1)} collective-permute-done((bf16[128,4096]{1,0:T(8,128)(2,1)S(1)}, bf16[128,4096]{1,0:T(8,128)(2,1)S(1)}, u32[]{:S(2)}, u32[]{:S(2)}) %collective-permute-start.4) | collective-permute-done | bytes 1048608 | tf_op jit(solution)/shard_map/ppermute | solution.py:263
  87.0 33.9 %all-to-all-done.2 = bf16[8,12,32,128]{3,2,1,0:T(8,128)(2,1)S(1)} async-done(((bf16[8,12,32,128]{3,2,1,0:T(8,128)(2,1)}), bf16[8,12,32,128]{3,2,1,0:T(8,128)(2,1)S(1)}, u32[]{:S(2)}, u32[]{:S(2)}) %all-to-all-start.2) | async-done | bytes 786464 | tf_op jit(solution)/shard_map/all_to_all | solution.py:275
  120.9 2.2 %shard_map.115 = bf16[64,32,128]{2,1,0:T(8,128)(2,1)} custom-call(s32[2]{0:T(128)S(1)} %pad_add_fusion.1.me, s32[4,4]{1,0:T(4,128)S(1)} %copy-done.3, s32[64]{0:T(128)S(1)} %bitcast.20, bf16[96,32,128]{2,1,0:T(8,128)(2,1)S(1)} %bitcast.16, bf16[128,4096]{1,0:T(8,128)(2,1)S(1)} %collective-permute-done.4.handoff), custom_call_target="tpu_custom_call" | custom-call | bytes 1048576 | tf_op jit(solution)/shard_map/pallas_call | solution.py:276
  123.0 9.8 %all-to-all-start.3 = ((bf16[16,4,32,128]{3,2,1,0:T(8,128)(2,1)}), bf16[16,4,32,128]{3,2,1,0:T(8,128)(2,1)S(1)}, u32[]{:S(2)}, u32[]{:S(2)}) async-start(bf16[16,4,32,128]{3,2,1,0:T(8,128)(2,1)} %bitcast.11), calls=%async_computation.3 | async-start | bytes 1048576 | tf_op jit(solution)/shard_map/all_to_all | solution.py:282
  132.9 15.8 %all-to-all-done.3 = bf16[16,4,32,128]{3,2,1,0:T(8,128)(2,1)S(1)} async-done(((bf16[16,4,32,128]{3,2,1,0:T(8,128)(2,1)}), bf16[16,4,32,128]{3,2,1,0:T(8,128)(2,1)S(1)}, u32[]{:S(2)}, u32[]{:S(2)}) %all-to-all-start.3) | async-done | bytes 524320 | tf_op jit(solution)/shard_map/all_to_all | solution.py:282
  149.4 1.0 copy.13
  (29 shorter events, 4.8 us)
Async XLA Ops:
  0.6 22.7 %copy-start.7 = (s32[1,1,2048]{2,1,0:T(1,128)S(1)}, s32[1,1,2048]{2,1,0:T(1,128)}, u32[]{:S(2)}) copy-start(s32[1,1,2048]{2,1,0:T(1,128)} %param.15) | copy-start | bytes 24580
  0.6 38.3 %copy-start.3 = (s32[4,4]{1,0:T(4,128)S(1)}, s32[4,4]{1,0:T(4,128)}, u32[]{:S(2)}) copy-start(s32[4,4]{1,0:T(4,128)} %recv.7) | copy-start | bytes 196
  0.7 38.3 %copy-start.4 = (s32[1,1,64]{2,1,0:T(1,128)S(1)}, s32[1,1,64]{2,1,0:T(1,128)}, u32[]{:S(2)}) copy-start(s32[1,1,64]{2,1,0:T(1,128)} %param.14) | copy-start | bytes 772
  0.7 0.7 copy-start.5
  4.8 19.5 %copy-start.6 = (bf16[32,4096]{1,0:T(8,128)(2,1)}, bf16[32,4096]{1,0:T(8,128)(2,1)S(1)}, u32[]{:S(2)}) copy-start(bf16[32,4096]{1,0:T(8,128)(2,1)S(1)} %get-tuple-element.23) | copy-start | bytes 786436
  4.8 34.1 %all-to-all-start = ((bf16[64,32,128]{2,1,0:T(8,128)(2,1)}), bf16[64,32,128]{2,1,0:T(8,128)(2,1)S(1)}, u32[]{:S(2)}, u32[]{:S(2)}) async-start(bf16[64,32,128]{2,1,0:T(8,128)(2,1)} %get-tuple-element.21), calls=%async_computation | async-start | bytes 1048576 | tf_op jit(solution)/shard_map/all_to_all | solution.py:239
  16.9 19.4 %collective-permute-start = (bf16[32,9216]{1,0:T(8,128)(2,1)}, bf16[32,9216]{1,0:T(8,128)(2,1)S(1)}, u32[]{:S(2)}, u32[]{:S(2)}) collective-permute-start(bf16[32,9216]{1,0:T(8,128)(2,1)} %get-tuple-element.18), channel_id=1, source_target_pairs={{0,128},{128,256},{256,384},{384,0},{1,129},{129,257},{257,385},{3... | collective-permute-start | bytes 1769480 | tf_op jit(solution)/shard_map/ppermute | solution.py:242
  20.4 18.6 %collective-permute-start.2 = (bf16[32,9216]{1,0:T(8,128)(2,1)S(1)}, bf16[32,9216]{1,0:T(8,128)(2,1)S(1)}, u32[]{:S(2)}, u32[]{:S(2)}) collective-permute-start(bf16[32,9216]{1,0:T(8,128)(2,1)S(1)} %get-tuple-element.20), channel_id=1, source_target_pairs={{0,384},{128,0},{256,128},{384,256},{1,385},{129,1},{257,129},{385... | collective-permute-start | bytes 1769480 | tf_op jit(solution)/shard_map/ppermute | solution.py:243
  40.7 19.3 %all-to-all-start.1 = ((bf16[8,12,32,128]{3,2,1,0:T(8,128)(2,1)}), bf16[8,12,32,128]{3,2,1,0:T(8,128)(2,1)S(1)}, u32[]{:S(2)}, u32[]{:S(2)}) async-start(bf16[8,12,32,128]{3,2,1,0:T(8,128)(2,1)} %shard_map.112), calls=%async_computation.1 | async-start | bytes 1572864 | tf_op jit(solution)/shard_map/all_to_all | solution.py:252
  45.8 14.2 %collective-permute-start.1 = (bf16[32,5120]{1,0:T(8,128)(2,1)}, bf16[32,5120]{1,0:T(8,128)(2,1)S(1)}, u32[]{:S(2)}, u32[]{:S(2)}) collective-permute-start(bf16[32,5120]{1,0:T(8,128)(2,1)} %get-tuple-element.19), channel_id=1, source_target_pairs={{0,256},{128,384},{256,0},{384,128},{1,257},{129,385},{257,1},{385... | collective-permute-start | bytes 983048 | tf_op jit(solution)/shard_map/ppermute | solution.py:244
  49.4 15.4 %collective-permute-start.5 = (bf16[32,4096]{1,0:T(8,128)(2,1)}, bf16[32,4096]{1,0:T(8,128)(2,1)S(1)}, u32[]{:S(2)}, u32[]{:S(2)}) collective-permute-start(bf16[32,4096]{1,0:T(8,128)(2,1)} %copy-done.6), channel_id=1, source_target_pairs={{0,256},{128,384},{256,0},{384,128},{1,257},{129,385},{257,1},{385... | collective-permute-start | bytes 786440 | tf_op jit(solution)/shard_map/ppermute | solution.py:245
  63.1 14.9 %collective-permute-start.3 = (bf16[128,4096]{1,0:T(8,128)(2,1)}, bf16[128,4096]{1,0:T(8,128)(2,1)}, u32[]{:S(2)}, u32[]{:S(2)}) collective-permute-start(bf16[128,4096]{1,0:T(8,128)(2,1)} %get-tuple-element.22), channel_id=1, source_target_pairs={{1,3},{3,5},{5,7},{7,1},{9,11},{11,13},{13,15},{15,9},{17,19},{19,... | collective-permute-start | bytes 3145736 | tf_op jit(solution)/shard_map/ppermute | solution.py:262
  64.8 0.7 copy-start.1
  65.5 0.9 copy-start.2
  71.4 0.9 copy-start
  72.3 48.6 %all-to-all-start.2 = ((bf16[8,12,32,128]{3,2,1,0:T(8,128)(2,1)}), bf16[8,12,32,128]{3,2,1,0:T(8,128)(2,1)S(1)}, u32[]{:S(2)}, u32[]{:S(2)}) async-start(bf16[8,12,32,128]{3,2,1,0:T(8,128)(2,1)} %copy-done), calls=%async_computation.2 | async-start | bytes 1572864 | tf_op jit(solution)/shard_map/all_to_all | solution.py:275
  79.3 7.6 %collective-permute-start.4 = (bf16[128,4096]{1,0:T(8,128)(2,1)S(1)}, bf16[128,4096]{1,0:T(8,128)(2,1)S(1)}, u32[]{:S(2)}, u32[]{:S(2)}) collective-permute-start(bf16[128,4096]{1,0:T(8,128)(2,1)S(1)} %broadcast_select_fusion), channel_id=1, source_target_pairs={{0,1},{1,0},{2,3},{3,2},{4,5},{5,4},{6,7},{7,6},{8,9},{9,8},{10,11... | collective-permute-start | bytes 3145736 | tf_op jit(solution)/shard_map/ppermute | solution.py:263
  123.0 25.6 %all-to-all-start.3 = ((bf16[16,4,32,128]{3,2,1,0:T(8,128)(2,1)}), bf16[16,4,32,128]{3,2,1,0:T(8,128)(2,1)S(1)}, u32[]{:S(2)}, u32[]{:S(2)}) async-start(bf16[16,4,32,128]{3,2,1,0:T(8,128)(2,1)} %bitcast.11), calls=%async_computation.3 | async-start | bytes 1048576 | tf_op jit(solution)/shard_map/all_to_all | solution.py:282

commit v3 on v2

--- a/solution.py
+++ b/solution.py
@@ -19,9 +19,9 @@
 KW = KEY_VALUE_HEADS * HEAD_SIZE
 K_AT = QW
 V_AT = QW + KW
-G_AT = QW + 2 * KW
-PAYLOAD = 2 * QW + 2 * KW
+PAYLOAD = QW + 2 * KW
 PIECES = 2 * KEY_VALUE_HEADS
+SPLIT = 3
 BEHIND = 3
 ENTRIES = N_DP * BEHIND
 SCALE = HEAD_SIZE ** (-0.5)
@@ -63,20 +63,17 @@
     return pl.ds(pl.multiple_of(block * BLOCK_POSITIONS, BLOCK_POSITIONS), BLOCK_POSITIONS)
 
 
-def pack(me, send, q_ref, g_ref, k_ref, v_ref, pieces, own, plus, minus, far, far_g, k_rows, v_rows, sems):
+def pack(me, send, q_ref, g_ref, k_ref, v_ref, pieces, *refs):
+    mains, grads, (k_rows, v_rows, sems) = refs[:N_DP], refs[N_DP : 2 * N_DP], refs[2 * N_DP :]
     r = me[0]
     copies = [
         pltpu.make_async_copy(k_ref, k_rows, sems.at[0]),
         pltpu.make_async_copy(v_ref, v_rows, sems.at[1]),
     ]
-    for shift, main, grad in ((1, plus, plus), (3, minus, minus), (2, far, far_g), (0, own, own)):
+    for shift in (1, 3, 2, 0):
         source = rows(send[r, replica(r, shift)])
-        for ref, target, column in ((q_ref, main, 0), (g_ref, grad, 0 if shift == 2 else G_AT)):
-            copies.append(
-                pltpu.make_async_copy(
-                    ref.at[source], target.at[:, column : column + QW], sems.at[len(copies)]
-                )
-            )
+        for ref, target in ((q_ref, mains[shift].at[:, :QW]), (g_ref, grads[shift])):
+            copies.append(pltpu.make_async_copy(ref.at[source], target, sems.at[len(copies)]))
     for copy in copies:
         copy.start()
     copies[0].wait()
@@ -89,15 +86,15 @@
             part = source[rows(block), column : column + HEAD_SIZE]
             for c in range(piece, N_CTX, PIECES):
                 pieces[u * N_CTX + c] = part
-    for shift, target in ((1, plus), (3, minus), (2, far), (0, own)):
+    for shift, target in enumerate(mains):
         block = send[r, replica(r, shift)]
         target[:, K_AT:V_AT] = k_rows[rows(block), :]
-        target[:, V_AT:G_AT] = v_rows[rows(block), :]
+        target[:, V_AT:] = v_rows[rows(block), :]
     for copy in copies[2:]:
         copy.wait()
 
 
-def gather_windows(me, recv, stretch, held, plus, minus, docs, out_ref, where_of):
+def gather_windows(me, recv, stretch, held, after, before, out_ref, where_of):
     r = me[0]
     first = (me[1] // PIECES) * PIECES
     for u in range(N_DP):
@@ -113,7 +110,7 @@
                 out_ref[d, shift * BEHIND + m] = held[source]
 
 
-def sum_windows(me, recv, stretch, held, handoff, out_ref, where_of):
+def sum_windows(me, recv, stretch, held, out_ref, where_of):
     r = me[0]
     first = (me[1] // PIECES) * PIECES
     for position in range(NB):
@@ -167,12 +164,12 @@
         target[rows(slot), at : at + HEAD_SIZE] = tall[i * BLOCK_POSITIONS : (i + 1) * BLOCK_POSITIONS]
 
 
-def forward(me, recv, stretch, own_block, plus, far, minus, docs, win, *outs):
+def forward(me, recv, stretch, x0, x1, x2, x3, docs, win, attn_a, attn_b, probs_out):
     r = me[0]
     key_at = lax.broadcasted_iota(jnp.int32, (SPAN, SPAN), 0)
     query_at = lax.broadcasted_iota(jnp.int32, (SPAN, SPAN), 1) % BLOCK_POSITIONS
     causal = key_at <= query_at + BEHIND * BLOCK_POSITIONS
-    for shift, x in enumerate((own_block, plus, far, minus)):
+    for shift, x in enumerate((x0, x1, x2, x3)):
         slot = recv[r, replica(r, -shift)]
         row = docs[pl.ds(stretch[me[1] * N_DP + slot], 1), :]
         key_doc = jnp.transpose(jnp.broadcast_to(row, (SPAN, SPAN)))
@@ -185,20 +182,20 @@
             logits = dot(key, stacked(x, 0, head), (1, 1)) * (SCALE * LOG2_E) + bias
             weights = jnp.exp2(logits - jnp.max(logits, axis=0, keepdims=True))
             probs = weights * (1.0 / jnp.sum(weights, axis=0, keepdims=True))
-            outs[-1][shift * KEY_VALUE_HEADS + head] = probs
+            probs_out[shift * KEY_VALUE_HEADS + head] = probs
             out = dot(probs.astype(jnp.bfloat16), value, (0, 0)).astype(jnp.bfloat16)
-            unstack(outs[0], slot, head, out)
-
-
-def backward(me, recv, own_block, plus, far, minus, far_g, win, probs_in, dq, sends, own):
-    r = me[0]
-    for shift, x in enumerate((own_block, plus, far, minus)):
+            unstack(attn_a if head < SPLIT else attn_b, slot, head if head < SPLIT else head - SPLIT, out)
+
+
+def backward(me, recv, x0, x1, x2, x3, y0, y1, y2, y3, win, probs_in, dq, sends, own):
+    r = me[0]
+    for shift, (x, y) in enumerate(((x0, y0), (x1, y1), (x2, y2), (x3, y3))):
         slot = recv[r, replica(r, -shift)]
         for head in range(KEY_VALUE_HEADS):
             key = window_of(win, x, shift, head, K_AT + head * HEAD_SIZE)
             value = window_of(win, x, shift, head + KEY_VALUE_HEADS, V_AT + head * HEAD_SIZE)
             query = stacked(x, 0, head)
-            grad = stacked(far_g, 0, head) if shift == 2 else stacked(x, G_AT, head)
+            grad = stacked(y, 0, head)
             probs = probs_in[shift * KEY_VALUE_HEADS + head]
             low = probs.astype(jnp.bfloat16)
             dprob = dot(value, grad, (1, 1))
@@ -215,6 +212,22 @@
                 own[rows(slot), column * HEAD_SIZE : (column + 1) * HEAD_SIZE] = term[BEHIND * BLOCK_POSITIONS :]
 
 
+def hold(kept, kept_too, arrived, *outs):
+    pass
+
+
+def stage(slots, body, shapes, *operands):
+    def never(*operands):
+        blank = [jnp.zeros(x.shape, x.dtype) for x in shapes]
+        return blank[0] if len(blank) == 1 else blank
+
+    def always(*operands):
+        result = body(*operands)
+        return list(result) if isinstance(result, (list, tuple)) else result
+
+    return lax.cond(slots[0, 0] >= 0, always, never, *operands)
+
+
 def window_docs(docs):
     padded = jnp.concatenate([jnp.full((BEHIND * BLOCK_POSITIONS,), -1, jnp.int32), docs])
     padded = padded.reshape(NB + BEHIND, BLOCK_POSITIONS)
@@ -228,61 +241,76 @@
     tokens = q.shape[0]
     n_section = lax.axis_size("section")
 
-    pieces, own_block, plus, minus, far, far_g = call(
+    pieces, *payloads = call(
         pack,
         [bf16(N_DP * N_CTX, BLOCK_POSITIONS, HEAD_SIZE)]
-        + [bf16(BLOCK_POSITIONS, width) for width in (PAYLOAD, PAYLOAD, PAYLOAD, G_AT, QW)],
+        + [bf16(BLOCK_POSITIONS, PAYLOAD)] * N_DP
+        + [bf16(BLOCK_POSITIONS, QW)] * N_DP,
         [SMEM, SMEM] + [ANY] * 4,
         [pltpu.VMEM((tokens, KW), jnp.bfloat16)] * 2 + [pltpu.SemaphoreType.DMA((2 + 2 * N_DP,))],
         nbytes=9 << 19,
     )(me, send_slot, *(pltpu.with_memory_space_constraint(x, pltpu.HBM) for x in (q, g, k, v)))
     held = lax.all_to_all(pieces, ("dp", "ctx"), 0, 0, tiled=True)
-    ahead = [(i, (i + 1) % N_DP) for i in range(N_DP)]
-    behind = [(i, (i - 1) % N_DP) for i in range(N_DP)]
-    plus = lax.ppermute(plus, "dp", ahead)
-    minus = lax.ppermute(minus, "dp", behind)
-    far = lax.ppermute(far, "dp", [(i, (i + 2) % N_DP) for i in range(N_DP)])
-    far_g = lax.ppermute(far_g, "dp", [(i, (i + 2) % N_DP) for i in range(N_DP)])
+    for at in range(2 * N_DP):
+        if at % N_DP:
+            route = [(i, (i + at) % N_DP) for i in range(N_DP)]
+            payloads[at] = lax.ppermute(payloads[at], "dp", route)
+    blocks, grads = payloads[:N_DP], payloads[N_DP:]
+    table = [pltpu.SMEM((NB,), jnp.int32)]
+    halves = [list(range(at, at + PIECES)) for at in range(0, N_CTX, PIECES)]
+    entries = bf16(PIECES, ENTRIES, BLOCK_POSITIONS, HEAD_SIZE)
+    group = bf16(NB, BLOCK_POSITIONS, HEAD_SIZE)
+    wanted = call(gather_windows, entries, [SMEM] * 3 + [VMEM] + [ANY] * 2, table)(
+        me, recv_slot, stretch, held, blocks[1], blocks[3]
+    )
+    windows = lax.all_to_all(wanted, "ctx", 0, 0, tiled=True, axis_index_groups=halves)
     docs = window_docs(doc_ids[0, 0])
-    table = [pltpu.SMEM((NB,), jnp.int32)]
-    wanted = call(
-        gather_windows, bf16(PIECES, ENTRIES, BLOCK_POSITIONS, HEAD_SIZE), [SMEM] * 3 + [VMEM] + [ANY] * 3, table
-    )(me, recv_slot, stretch, held, plus, minus, docs)
-    halves = [list(range(at, at + PIECES)) for at in range(0, N_CTX, PIECES)]
-    windows = lax.all_to_all(wanted, "ctx", 0, 0, tiled=True, axis_index_groups=halves)
-    attn, probs = call(
+    attn_a, attn_b, probs = call(
         forward,
-        [bf16(tokens, QW), jax.ShapeDtypeStruct((N_DP * KEY_VALUE_HEADS, SPAN, GROUP * BLOCK_POSITIONS), jnp.float32)],
+        [bf16(tokens, SPLIT * HEAD_SIZE * GROUP), bf16(tokens, QW - SPLIT * HEAD_SIZE * GROUP)]
+        + [jax.ShapeDtypeStruct((N_DP * KEY_VALUE_HEADS, SPAN, GROUP * BLOCK_POSITIONS), jnp.float32)],
         [SMEM] * 3 + [VMEM] * 6,
         flops=1 << 29,
         nbytes=6 << 20,
-    )(me, recv_slot, stretch, own_block, plus, far, minus, docs, windows)
+    )(me, recv_slot, stretch, *blocks, docs, windows)
     onward = [(i, (i + 1) % n_section) for i in range(n_section)]
-    odd = lax.axis_index("section") % 2 == 1
-    hop = lax.ppermute(attn, "section", [(i, (i + 2) % n_section) for i in range(1, n_section, 2)])
-    handoff = lax.ppermute(jnp.where(odd, hop, attn), "section", [(i, i ^ 1) for i in range(n_section)])
-    q_grad, sends, own = call(
-        backward,
-        [
-            bf16(tokens, QW),
-            bf16(PIECES, ENTRIES, BLOCK_POSITIONS, HEAD_SIZE),
-            jax.ShapeDtypeStruct((tokens, 2 * KW), jnp.float32),
-        ],
-        [SMEM] * 2 + [VMEM] * 7,
-        flops=1 << 30,
-        nbytes=6 << 20,
-    )(me, recv_slot, own_block, plus, far, minus, far_g, windows, probs)
-    partial = lax.all_to_all(sends, "ctx", 0, 0, tiled=True, axis_index_groups=halves)
-    summed = call(
-        sum_windows,
-        bf16(NB, BLOCK_POSITIONS, HEAD_SIZE),
-        [SMEM] * 3 + [VMEM] + [ANY],
-        table,
-    )(me, recv_slot, stretch, partial.reshape(PIECES * ENTRIES, BLOCK_POSITIONS, HEAD_SIZE), handoff)
-    back = lax.all_to_all(summed.reshape(N_CTX, N_DP, BLOCK_POSITIONS, HEAD_SIZE), "ctx", 0, 0, tiled=True)
-    k_grad, v_grad = call(finish, [bf16(tokens, KW)] * 2, [VMEM] * 2)(
-        back.reshape(NB, BLOCK_POSITIONS, HEAD_SIZE), own
+    handoff_a = lax.ppermute(attn_a, "section", onward)
+
+    def sum_gradients(blocks, windows, probs):
+        q_grad, sends, own = call(
+            backward,
+            [bf16(tokens, QW), entries, jax.ShapeDtypeStruct((tokens, 2 * KW), jnp.float32)],
+            [SMEM] * 2 + [VMEM] * 10,
+            flops=1 << 30,
+            nbytes=6 << 20,
+        )(me, recv_slot, *blocks, windows, probs)
+        partial = lax.all_to_all(sends, "ctx", 0, 0, tiled=True, axis_index_groups=halves)
+        summed = call(sum_windows, group, [SMEM] * 3 + [VMEM], table)(
+            me, recv_slot, stretch, partial.reshape(PIECES * ENTRIES, BLOCK_POSITIONS, HEAD_SIZE)
+        )
+        return q_grad, summed, own
+
+    q_grad, summed, own = stage(
+        send_slot,
+        sum_gradients,
+        [bf16(tokens, QW), group, jax.ShapeDtypeStruct((tokens, 2 * KW), jnp.float32)],
+        payloads,
+        windows,
+        probs,
     )
+    summed, attn_b = call(
+        hold, [group, bf16(*attn_b.shape)], [ANY] * 3, out_space=ANY, aliases={0: 0, 1: 1}
+    )(summed, attn_b, handoff_a)
+    handoff_b = lax.ppermute(attn_b, "section", onward)
+
+    def own_gradients(summed, own):
+        back = lax.all_to_all(summed.reshape(N_CTX, N_DP, BLOCK_POSITIONS, HEAD_SIZE), "ctx", 0, 0, tiled=True)
+        return call(finish, [bf16(tokens, KW)] * 2, [VMEM] * 2)(
+            back.reshape(NB, BLOCK_POSITIONS, HEAD_SIZE), own
+        )
+
+    k_grad, v_grad = stage(send_slot, own_gradients, [bf16(tokens, KW)] * 2, summed, own)
+    handoff = jnp.concatenate([handoff_a, handoff_b], axis=1)
     return handoff[None, None], q_grad[None, None], k_grad[None, None], v_grad[None, None]
 
 

time: 151 us -> 142 us (0.940)
  the two profiles are of different devices: /device:TPU:2 before, /device:TPU:65 now
where the time goes in v3:
time: 142 us
  starting transfers between devices  52.7 us (37%)
  blocking collectives  47.6 us (34%)
  waiting for transfers between devices  18.2 us (13%)
  Pallas kernels  15.5 us (11%)
  local copies, waits for them, and re-layouts  4.22 us (3%)
  other arithmetic  1.89 us (1%)
  between operations  1.46 us (1%)
    all_to_all x1, blocking collectives, own_gradients(): lax.all_to_all(summed.reshape(N_CTX, N_DP, BLOCK_POSITIONS, HEAD_SIZE), '...  25.6 us
    all_to_all x1, blocking collectives, sum_gradients(): lax.all_to_all(sends, 'ctx', 0, 0, tiled=True, axis_index_groups=halves)  22 us
    ppermute x6, starting transfers between devices, on_device(): payloads[at] = lax.ppermute(payloads[at], 'dp', route)  20.9 us
    ppermute x6, waiting for transfers between devices, on_device(): payloads[at] = lax.ppermute(payloads[at], 'dp', route)  18.2 us
    ppermute x1, starting transfers between devices, on_device(): handoff_a = lax.ppermute(attn_a, 'section', onward)  11 us
    all_to_all x1, starting transfers between devices, on_device(): held = lax.all_to_all(pieces, ('dp', 'ctx'), 0, 0, tiled=True)  10.7 us
    ppermute x1, starting transfers between devices, on_device(): handoff_b = lax.ppermute(attn_b, 'section', onward)  5.65 us
    pallas_call x1, Pallas kernels, sum_gradients(): call(backward, [bf16(tokens, QW), entries, jax.ShapeDtypeStruct((tokens,...  5.64 us
  transfers between devices with their start and end apart: 10, of which 5 were waited for; matrix products, arithmetic and copies ran while one was open for 2% of the time, Pallas kernels for 5%

profile of v3, /device:TPU:65, one launch (start us, length us, event | category | flops | bytes accessed | tf_op | source)
XLA Modules:
  0.0 141.6 jit_solution(13720486567572349122)
XLA Ops:
  1.4 3.3 %shard_map.111 = (bf16[64,32,128]{2,1,0:T(8,128)(2,1)}, bf16[32,5120]{1,0:T(8,128)(2,1)}, bf16[32,5120]{1,0:T(8,128)(2,1)S(1)}, bf16[32,5120]{1,0:T(8,128)(2,1)S...) custom-call(s32[2]{0:T(128)S(1)} %pad_add_fusion.1.me, ...), custom_call_target="tpu_custom_call" | custom-call | bytes 4718592 | tf_op jit(solution)/shard_map/pallas_call | solution.py:244
  4.7 10.7 %all-to-all-start.2 = ((bf16[64,32,128]{2,1,0:T(8,128)(2,1)}), bf16[64,32,128]{2,1,0:T(8,128)(2,1)S(1)}, u32[]{:S(2)}, u32[]{:S(2)}) async-start(bf16[64,32,128]{2,1,0:T(8,128)(2,1)} %get-tuple-element.82), calls=%async_computation.2 | async-start | bytes 1048576 | tf_op jit(solution)/shard_map/all_to_all | solution.py:253
  15.4 3.1 %collective-permute-start = (bf16[32,5120]{1,0:T(8,128)(2,1)S(1)}, bf16[32,5120]{1,0:T(8,128)(2,1)S(1)}, u32[]{:S(2)}, u32[]{:S(2)}) collective-permute-start(bf16[32,5120]{1,0:T(8,128)(2,1)S(1)} %get-tuple-element.79), channel_id=1, source_target_pairs={{0,128},{128,256},{256,384},{384,0},{1,129},{129,257},{257,385},{3... | collective-permute-start | bytes 983048 | tf_op jit(solution)/shard_map/ppermute | solution.py:257
  18.5 3.4 %collective-permute-start.2 = (bf16[32,5120]{1,0:T(8,128)(2,1)S(1)}, bf16[32,5120]{1,0:T(8,128)(2,1)S(1)}, u32[]{:S(2)}, u32[]{:S(2)}) collective-permute-start(bf16[32,5120]{1,0:T(8,128)(2,1)S(1)} %get-tuple-element.81), channel_id=1, source_target_pairs={{0,384},{128,0},{256,128},{384,256},{1,385},{129,1},{257,129},{385... | collective-permute-start | bytes 983048 | tf_op jit(solution)/shard_map/ppermute | solution.py:257
  21.9 9.7 %collective-permute-done.after.x1 = bf16[32,5120]{1,0:T(8,128)(2,1)S(1)} collective-permute-done((bf16[32,5120]{1,0:T(8,128)(2,1)S(1)}, bf16[32,5120]{1,0:T(8,128)(2,1)S(1)}, u32[]{:S(2)}, u32[]{:S(2)}) %collective-permute-start) | collective-permute-done | bytes 327712 | tf_op jit(solution)/shard_map/ppermute | solution.py:257
  32.6 1.7 %shard_map.112 = bf16[8,12,32,128]{3,2,1,0:T(8,128)(2,1)} custom-call(s32[2]{0:T(128)S(1)} %pad_add_fusion.1.me, s32[4,4]{1,0:T(4,128)S(1)} %copy-done.7, s32[64]{0:T(128)S(1)} %bitcast.28, bf16[64,32,128]{2,1,0:T(8,128)(2,1)S(1)} %all-to-all-done.2.held, bf16[32,5120]{1,0:T(8,128)(2,1)} %copy-done.1, bf16[32,5120]{1,0:T(8,128)(2,1)} %copy-done.3), custom_call_target="tpu_custom_call" | custom-call | bytes 1048576 | tf_op jit(solution)/shard_map/pallas_call | solution.py:263
  34.3 4.6 %all-to-all-start.3 = ((bf16[8,12,32,128]{3,2,1,0:T(8,128)(2,1)}), bf16[8,12,32,128]{3,2,1,0:T(8,128)(2,1)S(1)}, u32[]{:S(2)}, u32[]{:S(2)}) async-start(bf16[8,12,32,128]{3,2,1,0:T(8,128)(2,1)} %shard_map.112), calls=%async_computation.3 | async-start | bytes 1572864 | tf_op jit(solution)/shard_map/all_to_all | solution.py:266
  38.9 4.2 %collective-permute-start.1 = (bf16[32,5120]{1,0:T(8,128)(2,1)S(1)}, bf16[32,5120]{1,0:T(8,128)(2,1)S(1)}, u32[]{:S(2)}, u32[]{:S(2)}) collective-permute-start(bf16[32,5120]{1,0:T(8,128)(2,1)S(1)} %get-tuple-element.80), channel_id=1, source_target_pairs={{0,256},{128,384},{256,0},{384,128},{1,257},{129,385},{257,1},{385... | collective-permute-start | bytes 983048 | tf_op jit(solution)/shard_map/ppermute | solution.py:257
  44.8 5.3 %collective-permute-done.1.x2 = bf16[32,5120]{1,0:T(8,128)(2,1)S(1)} collective-permute-done((bf16[32,5120]{1,0:T(8,128)(2,1)S(1)}, bf16[32,5120]{1,0:T(8,128)(2,1)S(1)}, u32[]{:S(2)}, u32[]{:S(2)}) %collective-permute-start.1) | collective-permute-done | bytes 327712 | tf_op jit(solution)/shard_map/ppermute | solution.py:257
  50.8 2.6 %shard_map.113 = (bf16[128,3072]{1,0:T(8,128)(2,1)S(1)}, bf16[128,1024]{1,0:T(8,128)(2,1)S(1)}, f32[16,128,256]{2,1,0:T(8,128)S(1)}) custom-call(s32[2]{0:T(128)S(1)} %pad_add_fusion.1.me, s32[4,4]{1,0:T(4,128)S(1)} %copy-done.7, s32[64]{0:T(128)S(1)} %bitcast.29, bf16[32,5120]{1,0:T(8,128)(2,1)} %get-tuple-element.78.x0, bf16[32,5120]{1,0:T(8,128)(2,1)S(1)} %copy-done.2, ...), custom_call_target="tpu_custom_call" | custom-call | flops 536870912 | bytes 6291456 | tf_op jit(solution)/shard_map/pallas_call | solution.py:268
  53.5 11.0 %collective-permute-start.3 = (bf16[128,3072]{1,0:T(8,128)(2,1)S(1)}, bf16[128,3072]{1,0:T(8,128)(2,1)S(1)}, u32[]{:S(2)}, u32[]{:S(2)}) collective-permute-start(bf16[128,3072]{1,0:T(8,128)(2,1)S(1)} %get-tuple-element.83), channel_id=1, source_target_pairs={{0,1},{1,2},{2,3},{3,4},{4,5},{5,6},{6,7},{7,0},{8,9},{9,10},{10,1... | collective-permute-start | bytes 2359304 | tf_op jit(solution)/shard_map/ppermute | solution.py:277
  64.5 3.0 %collective-permute-start.4 = (bf16[32,4096]{1,0:T(8,128)(2,1)S(1)}, bf16[32,4096]{1,0:T(8,128)(2,1)S(1)}, u32[]{:S(2)}, u32[]{:S(2)}) collective-permute-start(bf16[32,4096]{1,0:T(8,128)(2,1)S(1)} %get-tuple-element.85), channel_id=1, source_target_pairs={{0,128},{128,256},{256,384},{384,0},{1,129},{129,257},{257,385},{3... | collective-permute-start | bytes 786440 | tf_op jit(solution)/shard_map/ppermute | solution.py:257
  67.5 4.5 %collective-permute-start.5 = (bf16[32,4096]{1,0:T(8,128)(2,1)S(1)}, bf16[32,4096]{1,0:T(8,128)(2,1)S(1)}, u32[]{:S(2)}, u32[]{:S(2)}) collective-permute-start(bf16[32,4096]{1,0:T(8,128)(2,1)S(1)} %get-tuple-element.86), channel_id=1, source_target_pairs={{0,256},{128,384},{256,0},{384,128},{1,257},{129,385},{257,1},{385... | collective-permute-start | bytes 786440 | tf_op jit(solution)/shard_map/ppermute | solution.py:257
  72.0 2.6 %collective-permute-start.6 = (bf16[32,4096]{1,0:T(8,128)(2,1)S(1)}, bf16[32,4096]{1,0:T(8,128)(2,1)S(1)}, u32[]{:S(2)}, u32[]{:S(2)}) collective-permute-start(bf16[32,4096]{1,0:T(8,128)(2,1)S(1)} %get-tuple-element.87), channel_id=1, source_target_pairs={{0,384},{128,0},{256,128},{384,256},{1,385},{129,1},{257,129},{385... | collective-permute-start | bytes 786440 | tf_op jit(solution)/shard_map/ppermute | solution.py:257
  74.7 1.2 slice.59
  76.9 2.5 %collective-permute-done.6 = bf16[32,4096]{1,0:T(8,128)(2,1)S(1)} collective-permute-done((bf16[32,4096]{1,0:T(8,128)(2,1)S(1)}, bf16[32,4096]{1,0:T(8,128)(2,1)S(1)}, u32[]{:S(2)}, u32[]{:S(2)}) %collective-permute-start.6) | collective-permute-done | bytes 262176 | tf_op jit(solution)/shard_map/ppermute | solution.py:257
  79.4 29.0 %conditional.2 = (bf16[64,32,128]{2,1,0:T(8,128)(2,1)S(1)}, f32[128,1024]{1,0:T(8,128)S(1)}, bf16[1,1,128,4096]{3,2,1,0:T(8,128)(2,1)}) conditional(s32[]{:T(128)} %bitcast.14, () %tuple.30, (s32[2]{0:T(128)S(1)}, s32[4,4]{1,0:T(4,128)S(1)}, bf16[32,5120]{1,0:T(8,128)(2,1)}, bf16[32,5120]{1,0:T(8,128)(2,1)}, bf16[32,5120]{1,0:T(8,128)(2,1)S(1)}, ...), branch_computations={%region_0.0_spmd, %region_1.0_spmd} | conditional | flops 1073741824 | bytes 8912920 | solution.py:228
  79.4 5.6 %branch_1_fun.3 = (bf16[128,4096]{1,0:T(8,128)(2,1)}, bf16[8,12,32,128]{3,2,1,0:T(8,128)(2,1)S(1)}, f32[128,1024]{1,0:T(8,128)S(1)}) custom-call(s32[2]{0:T(128)S(1)} %get-tuple-element.35.me, s32[4,4]{1,0:T(4,128)S(1)} %get-tuple-element.36.recv, bf16[32,5120]{1,0:T(8,128)(2,1)} %get-tuple-element.38.x0, bf16[32,5120]{1,0:T(8,128)(2,1)} %get-tuple-element.39.x1, ...), custom_call_target="tpu_custom_call" | custom-call | flops 1073741824 | bytes 6291456 | tf_op jit(solution)/shard_map/cond/branch_1_fun/pallas_call | solution.py:280
  85.1 22.0 %all_to_all.18 = bf16[8,12,32,128]{3,2,1,0:T(8,128)(2,1)S(1)} all-to-all(bf16[8,12,32,128]{3,2,1,0:T(8,128)(2,1)S(1)} %get-tuple-element.48), channel_id=1, replica_groups={{0,8,16,24,32,40,48,56},{64,72,80,88,96,104,112,120},{1,9,17,25,33,41,4..., dimensions={0} | all-to-all | bytes 1572864 | tf_op jit(solution)/shard_map/cond/branch_1_fun/all_to_all | solution.py:287
  107.1 1.4 branch_1_fun.4
  108.5 5.6 %collective-permute-start.7 = (bf16[128,1024]{1,0:T(8,128)(2,1)S(1)}, bf16[128,1024]{1,0:T(8,128)(2,1)S(1)}, u32[]{:S(2)}, u32[]{:S(2)}) collective-permute-start(bf16[128,1024]{1,0:T(8,128)(2,1)S(1)} %get-tuple-element.91), channel_id=1, source_target_pairs={{0,1},{1,2},{2,3},{3,4},{4,5},{5,6},{6,7},{7,0},{8,9},{9,10},{10,1... | collective-permute-start | bytes 786440 | tf_op jit(solution)/shard_map/ppermute | solution.py:304
  114.2 26.4 %conditional.3 = (bf16[1,1,128,512]{3,2,1,0:T(8,128)(2,1)}, bf16[1,1,128,512]{3,2,1,0:T(8,128)(2,1)}) conditional(s32[]{:T(128)} %bitcast.14, () %tuple.32, (bf16[64,32,128]{2,1,0:T(8,128)(2,1)S(1)}, f32[128,1024]{1,0:T(8,128)S(1)}) %tuple.33), branch_computations={%region_2.0_spmd, %region_3.0_spmd} | conditional | bytes 2097168 | solution.py:228
  114.2 25.6 %all_to_all.19 = bf16[16,4,32,128]{3,2,1,0:T(8,128)(2,1)S(1)} all-to-all(bf16[16,4,32,128]{3,2,1,0:T(8,128)(2,1)S(1)} %bitcast.19), channel_id=1, replica_groups=mesh['dp'=4,'ctx'=16,'section'=8] {'ctx'}, dimensions={0} | all-to-all | bytes 1048576 | tf_op jit(solution)/shard_map/cond/branch_1_fun/all_to_all | solution.py:307
  140.6 1.0 maximum_bitcast_fusion
  (38 shorter events, 5.3 us)
Async XLA Ops:
  0.6 32.0 %copy-start.7 = (s32[4,4]{1,0:T(4,128)S(1)}, s32[4,4]{1,0:T(4,128)}, u32[]{:S(2)}) copy-start(s32[4,4]{1,0:T(4,128)} %recv.3) | copy-start | bytes 196
  0.6 31.9 %copy-start.9 = (s32[1,1,64]{2,1,0:T(1,128)S(1)}, s32[1,1,64]{2,1,0:T(1,128)}, u32[]{:S(2)}) copy-start(s32[1,1,64]{2,1,0:T(1,128)} %param.18) | copy-start | bytes 772
  0.7 0.7 copy-start
  4.7 39.0 %copy-start.8 = (s32[1,1,2048]{2,1,0:T(1,128)S(1)}, s32[1,1,2048]{2,1,0:T(1,128)}, u32[]{:S(2)}) copy-start(s32[1,1,2048]{2,1,0:T(1,128)} %param.19) | copy-start | bytes 24580
  4.7 27.2 %all-to-all-start.2 = ((bf16[64,32,128]{2,1,0:T(8,128)(2,1)}), bf16[64,32,128]{2,1,0:T(8,128)(2,1)S(1)}, u32[]{:S(2)}, u32[]{:S(2)}) async-start(bf16[64,32,128]{2,1,0:T(8,128)(2,1)} %get-tuple-element.82), calls=%async_computation.2 | async-start | bytes 1048576 | tf_op jit(solution)/shard_map/all_to_all | solution.py:253
  15.4 16.2 %collective-permute-start = (bf16[32,5120]{1,0:T(8,128)(2,1)S(1)}, bf16[32,5120]{1,0:T(8,128)(2,1)S(1)}, u32[]{:S(2)}, u32[]{:S(2)}) collective-permute-start(bf16[32,5120]{1,0:T(8,128)(2,1)S(1)} %get-tuple-element.79), channel_id=1, source_target_pairs={{0,128},{128,256},{256,384},{384,0},{1,129},{129,257},{257,385},{3... | collective-permute-start | bytes 983048 | tf_op jit(solution)/shard_map/ppermute | solution.py:257
  18.5 13.3 %collective-permute-start.2 = (bf16[32,5120]{1,0:T(8,128)(2,1)S(1)}, bf16[32,5120]{1,0:T(8,128)(2,1)S(1)}, u32[]{:S(2)}, u32[]{:S(2)}) collective-permute-start(bf16[32,5120]{1,0:T(8,128)(2,1)S(1)} %get-tuple-element.81), channel_id=1, source_target_pairs={{0,384},{128,0},{256,128},{384,256},{1,385},{129,1},{257,129},{385... | collective-permute-start | bytes 983048 | tf_op jit(solution)/shard_map/ppermute | solution.py:257
  31.6 0.7 copy-start.1
  31.9 0.7 copy-start.3
  34.3 16.5 %copy-start.2 = (bf16[32,5120]{1,0:T(8,128)(2,1)S(1)}, bf16[32,5120]{1,0:T(8,128)(2,1)}, u32[]{:S(2)}) copy-start(bf16[32,5120]{1,0:T(8,128)(2,1)} %copy-done.1) | copy-start | bytes 983044
  34.3 16.5 %copy-start.4 = (bf16[32,5120]{1,0:T(8,128)(2,1)S(1)}, bf16[32,5120]{1,0:T(8,128)(2,1)}, u32[]{:S(2)}) copy-start(bf16[32,5120]{1,0:T(8,128)(2,1)} %copy-done.3) | copy-start | bytes 983044
  34.3 15.8 %all-to-all-start.3 = ((bf16[8,12,32,128]{3,2,1,0:T(8,128)(2,1)}), bf16[8,12,32,128]{3,2,1,0:T(8,128)(2,1)S(1)}, u32[]{:S(2)}, u32[]{:S(2)}) async-start(bf16[8,12,32,128]{3,2,1,0:T(8,128)(2,1)} %shard_map.112), calls=%async_computation.3 | async-start | bytes 1572864 | tf_op jit(solution)/shard_map/all_to_all | solution.py:266
  38.9 11.2 %collective-permute-start.1 = (bf16[32,5120]{1,0:T(8,128)(2,1)S(1)}, bf16[32,5120]{1,0:T(8,128)(2,1)S(1)}, u32[]{:S(2)}, u32[]{:S(2)}) collective-permute-start(bf16[32,5120]{1,0:T(8,128)(2,1)S(1)} %get-tuple-element.80), channel_id=1, source_target_pairs={{0,256},{128,384},{256,0},{384,128},{1,257},{129,385},{257,1},{385... | collective-permute-start | bytes 983048 | tf_op jit(solution)/shard_map/ppermute | solution.py:257
  50.1 0.7 copy-start.5
  50.8 28.6 %copy-start.6 = (bf16[32,5120]{1,0:T(8,128)(2,1)S(1)}, bf16[32,5120]{1,0:T(8,128)(2,1)}, u32[]{:S(2)}) copy-start(bf16[32,5120]{1,0:T(8,128)(2,1)} %copy-done.5) | copy-start | bytes 983044
  53.5 55.0 %collective-permute-start.3 = (bf16[128,3072]{1,0:T(8,128)(2,1)S(1)}, bf16[128,3072]{1,0:T(8,128)(2,1)S(1)}, u32[]{:S(2)}, u32[]{:S(2)}) collective-permute-start(bf16[128,3072]{1,0:T(8,128)(2,1)S(1)} %get-tuple-element.83), channel_id=1, source_target_pairs={{0,1},{1,2},{2,3},{3,4},{4,5},{5,6},{6,7},{7,0},{8,9},{9,10},{10,1... | collective-permute-start | bytes 2359304 | tf_op jit(solution)/shard_map/ppermute | solution.py:277
  64.5 12.0 %collective-permute-start.4 = (bf16[32,4096]{1,0:T(8,128)(2,1)S(1)}, bf16[32,4096]{1,0:T(8,128)(2,1)S(1)}, u32[]{:S(2)}, u32[]{:S(2)}) collective-permute-start(bf16[32,4096]{1,0:T(8,128)(2,1)S(1)} %get-tuple-element.85), channel_id=1, source_target_pairs={{0,128},{128,256},{256,384},{384,0},{1,129},{129,257},{257,385},{3... | collective-permute-start | bytes 786440 | tf_op jit(solution)/shard_map/ppermute | solution.py:257
  67.5 9.4 %collective-permute-start.5 = (bf16[32,4096]{1,0:T(8,128)(2,1)S(1)}, bf16[32,4096]{1,0:T(8,128)(2,1)S(1)}, u32[]{:S(2)}, u32[]{:S(2)}) collective-permute-start(bf16[32,4096]{1,0:T(8,128)(2,1)S(1)} %get-tuple-element.86), channel_id=1, source_target_pairs={{0,256},{128,384},{256,0},{384,128},{1,257},{129,385},{257,1},{385... | collective-permute-start | bytes 786440 | tf_op jit(solution)/shard_map/ppermute | solution.py:257
  72.0 7.4 %collective-permute-start.6 = (bf16[32,4096]{1,0:T(8,128)(2,1)S(1)}, bf16[32,4096]{1,0:T(8,128)(2,1)S(1)}, u32[]{:S(2)}, u32[]{:S(2)}) collective-permute-start(bf16[32,4096]{1,0:T(8,128)(2,1)S(1)} %get-tuple-element.87), channel_id=1, source_target_pairs={{0,384},{128,0},{256,128},{384,256},{1,385},{129,1},{257,129},{385... | collective-permute-start | bytes 786440 | tf_op jit(solution)/shard_map/ppermute | solution.py:257
  108.5 32.1 %collective-permute-start.7 = (bf16[128,1024]{1,0:T(8,128)(2,1)S(1)}, bf16[128,1024]{1,0:T(8,128)(2,1)S(1)}, u32[]{:S(2)}, u32[]{:S(2)}) collective-permute-start(bf16[128,1024]{1,0:T(8,128)(2,1)S(1)} %get-tuple-element.91), channel_id=1, source_target_pairs={{0,1},{1,2},{2,3},{3,4},{4,5},{5,6},{6,7},{7,0},{8,9},{9,10},{10,1... | collective-permute-start | bytes 786440 | tf_op jit(solution)/shard_map/ppermute | solution.py:304

commit v4 on v3

--- a/solution.py
+++ b/solution.py
@@ -21,7 +21,7 @@
 V_AT = QW + KW
 PAYLOAD = QW + 2 * KW
 PIECES = 2 * KEY_VALUE_HEADS
-SPLIT = 3
+PARTS = ((0, 1), (2,), (3,))
 BEHIND = 3
 ENTRIES = N_DP * BEHIND
 SCALE = HEAD_SIZE ** (-0.5)
@@ -64,7 +64,7 @@
 
 
 def pack(me, send, q_ref, g_ref, k_ref, v_ref, pieces, *refs):
-    mains, grads, (k_rows, v_rows, sems) = refs[:N_DP], refs[N_DP : 2 * N_DP], refs[2 * N_DP :]
+    mains, (grads, k_rows, v_rows, sems) = refs[:N_DP], refs[N_DP:]
     r = me[0]
     copies = [
         pltpu.make_async_copy(k_ref, k_rows, sems.at[0]),
@@ -72,7 +72,7 @@
     ]
     for shift in (1, 3, 2, 0):
         source = rows(send[r, replica(r, shift)])
-        for ref, target in ((q_ref, mains[shift].at[:, :QW]), (g_ref, grads[shift])):
+        for ref, target in ((q_ref, mains[shift].at[:, :QW]), (g_ref, grads.at[replica(r, shift)])):
             copies.append(pltpu.make_async_copy(ref.at[source], target, sems.at[len(copies)]))
     for copy in copies:
         copy.start()
@@ -164,7 +164,7 @@
         target[rows(slot), at : at + HEAD_SIZE] = tall[i * BLOCK_POSITIONS : (i + 1) * BLOCK_POSITIONS]
 
 
-def forward(me, recv, stretch, x0, x1, x2, x3, docs, win, attn_a, attn_b, probs_out):
+def forward(me, recv, stretch, x0, x1, x2, x3, docs, win, *outs):
     r = me[0]
     key_at = lax.broadcasted_iota(jnp.int32, (SPAN, SPAN), 0)
     query_at = lax.broadcasted_iota(jnp.int32, (SPAN, SPAN), 1) % BLOCK_POSITIONS
@@ -182,24 +182,26 @@
             logits = dot(key, stacked(x, 0, head), (1, 1)) * (SCALE * LOG2_E) + bias
             weights = jnp.exp2(logits - jnp.max(logits, axis=0, keepdims=True))
             probs = weights * (1.0 / jnp.sum(weights, axis=0, keepdims=True))
-            probs_out[shift * KEY_VALUE_HEADS + head] = probs
-            out = dot(probs.astype(jnp.bfloat16), value, (0, 0)).astype(jnp.bfloat16)
-            unstack(attn_a if head < SPLIT else attn_b, slot, head if head < SPLIT else head - SPLIT, out)
-
-
-def backward(me, recv, x0, x1, x2, x3, y0, y1, y2, y3, win, probs_in, dq, sends, own):
-    r = me[0]
-    for shift, (x, y) in enumerate(((x0, y0), (x1, y1), (x2, y2), (x3, y3))):
+            low = probs.astype(jnp.bfloat16)
+            outs[-1][shift * KEY_VALUE_HEADS + head] = low
+            out = dot(low, value, (0, 0)).astype(jnp.bfloat16)
+            part = [head in heads for heads in PARTS].index(True)
+            unstack(outs[part], slot, PARTS[part].index(head), out)
+
+
+def backward(me, recv, x0, x1, x2, x3, grads, win, probs_in, dq, sends, own):
+    r = me[0]
+    for shift, x in enumerate((x0, x1, x2, x3)):
         slot = recv[r, replica(r, -shift)]
         for head in range(KEY_VALUE_HEADS):
             key = window_of(win, x, shift, head, K_AT + head * HEAD_SIZE)
             value = window_of(win, x, shift, head + KEY_VALUE_HEADS, V_AT + head * HEAD_SIZE)
             query = stacked(x, 0, head)
-            grad = stacked(y, 0, head)
-            probs = probs_in[shift * KEY_VALUE_HEADS + head]
-            low = probs.astype(jnp.bfloat16)
+            grad = stacked(grads.at[replica(r, -shift)], 0, head)
+            low = probs_in[shift * KEY_VALUE_HEADS + head]
+            probs = low.astype(jnp.float32)
             dprob = dot(value, grad, (1, 1))
-            delta = jnp.sum(low.astype(jnp.float32) * dprob, axis=0, keepdims=True)
+            delta = jnp.sum(probs * dprob, axis=0, keepdims=True)
             dlogit = (probs * (dprob - delta)).astype(jnp.bfloat16)
             unstack(dq, slot, head, (dot(dlogit, key, (0, 0)) * SCALE).astype(jnp.bfloat16))
             for column, term in (
@@ -212,11 +214,11 @@
                 own[rows(slot), column * HEAD_SIZE : (column + 1) * HEAD_SIZE] = term[BEHIND * BLOCK_POSITIONS :]
 
 
-def hold(kept, kept_too, arrived, *outs):
+def hold(kept, kept_too, arrived, arrived_too, *outs):
     pass
 
 
-def stage(slots, body, shapes, *operands):
+def stage(me, body, shapes, *operands):
     def never(*operands):
         blank = [jnp.zeros(x.shape, x.dtype) for x in shapes]
         return blank[0] if len(blank) == 1 else blank
@@ -225,7 +227,7 @@
         result = body(*operands)
         return list(result) if isinstance(result, (list, tuple)) else result
 
-    return lax.cond(slots[0, 0] >= 0, always, never, *operands)
+    return lax.cond(me[0] >= 0, always, never, *operands)
 
 
 def window_docs(docs):
@@ -245,17 +247,16 @@
         pack,
         [bf16(N_DP * N_CTX, BLOCK_POSITIONS, HEAD_SIZE)]
         + [bf16(BLOCK_POSITIONS, PAYLOAD)] * N_DP
-        + [bf16(BLOCK_POSITIONS, QW)] * N_DP,
+        + [bf16(N_DP, BLOCK_POSITIONS, QW)],
         [SMEM, SMEM] + [ANY] * 4,
         [pltpu.VMEM((tokens, KW), jnp.bfloat16)] * 2 + [pltpu.SemaphoreType.DMA((2 + 2 * N_DP,))],
         nbytes=9 << 19,
     )(me, send_slot, *(pltpu.with_memory_space_constraint(x, pltpu.HBM) for x in (q, g, k, v)))
     held = lax.all_to_all(pieces, ("dp", "ctx"), 0, 0, tiled=True)
-    for at in range(2 * N_DP):
-        if at % N_DP:
-            route = [(i, (i + at) % N_DP) for i in range(N_DP)]
-            payloads[at] = lax.ppermute(payloads[at], "dp", route)
-    blocks, grads = payloads[:N_DP], payloads[N_DP:]
+    grads = payloads[N_DP]
+    blocks = [payloads[0]] + [
+        lax.ppermute(payloads[at], "dp", [(i, (i + at) % N_DP) for i in range(N_DP)]) for at in range(1, N_DP)
+    ]
     table = [pltpu.SMEM((NB,), jnp.int32)]
     halves = [list(range(at, at + PIECES)) for at in range(0, N_CTX, PIECES)]
     entries = bf16(PIECES, ENTRIES, BLOCK_POSITIONS, HEAD_SIZE)
@@ -264,23 +265,29 @@
         me, recv_slot, stretch, held, blocks[1], blocks[3]
     )
     windows = lax.all_to_all(wanted, "ctx", 0, 0, tiled=True, axis_index_groups=halves)
+    grads = lax.all_to_all(grads, "dp", 0, 0, tiled=True)
     docs = window_docs(doc_ids[0, 0])
-    attn_a, attn_b, probs = call(
+    attn_a, attn_b, attn_c, probs = call(
         forward,
-        [bf16(tokens, SPLIT * HEAD_SIZE * GROUP), bf16(tokens, QW - SPLIT * HEAD_SIZE * GROUP)]
-        + [jax.ShapeDtypeStruct((N_DP * KEY_VALUE_HEADS, SPAN, GROUP * BLOCK_POSITIONS), jnp.float32)],
+        [bf16(tokens, len(heads) * HEAD_SIZE * GROUP) for heads in PARTS]
+        + [bf16(N_DP * KEY_VALUE_HEADS, SPAN, GROUP * BLOCK_POSITIONS)],
         [SMEM] * 3 + [VMEM] * 6,
         flops=1 << 29,
         nbytes=6 << 20,
     )(me, recv_slot, stretch, *blocks, docs, windows)
     onward = [(i, (i + 1) % n_section) for i in range(n_section)]
+    odd = range(1, n_section, 2)
+    around = [(i, (i - 2) % n_section) for i in odd]
+    last = [(i, (i - 3) % n_section) for i in odd] + [(i - 1, i) for i in odd]
     handoff_a = lax.ppermute(attn_a, "section", onward)
+    relay = lax.ppermute(attn_c, "section", around)
+    relay = lax.ppermute(relay, "section", around)
 
     def sum_gradients(blocks, windows, probs):
         q_grad, sends, own = call(
             backward,
             [bf16(tokens, QW), entries, jax.ShapeDtypeStruct((tokens, 2 * KW), jnp.float32)],
-            [SMEM] * 2 + [VMEM] * 10,
+            [SMEM] * 2 + [VMEM] * 7,
             flops=1 << 30,
             nbytes=6 << 20,
         )(me, recv_slot, *blocks, windows, probs)
@@ -291,17 +298,19 @@
         return q_grad, summed, own
 
     q_grad, summed, own = stage(
-        send_slot,
+        me,
         sum_gradients,
         [bf16(tokens, QW), group, jax.ShapeDtypeStruct((tokens, 2 * KW), jnp.float32)],
-        payloads,
+        [*blocks, grads],
         windows,
         probs,
     )
     summed, attn_b = call(
-        hold, [group, bf16(*attn_b.shape)], [ANY] * 3, out_space=ANY, aliases={0: 0, 1: 1}
-    )(summed, attn_b, handoff_a)
+        hold, [group, bf16(*attn_b.shape)], [ANY] * 4, out_space=ANY, aliases={0: 0, 1: 1}
+    )(summed, attn_b, handoff_a, relay)
     handoff_b = lax.ppermute(attn_b, "section", onward)
+    relay = jnp.where(lax.axis_index("section") % 2 == 1, relay, attn_c)
+    handoff_c = lax.ppermute(relay, "section", last)
 
     def own_gradients(summed, own):
         back = lax.all_to_all(summed.reshape(N_CTX, N_DP, BLOCK_POSITIONS, HEAD_SIZE), "ctx", 0, 0, tiled=True)
@@ -309,8 +318,8 @@
             back.reshape(NB, BLOCK_POSITIONS, HEAD_SIZE), own
         )
 
-    k_grad, v_grad = stage(send_slot, own_gradients, [bf16(tokens, KW)] * 2, summed, own)
-    handoff = jnp.concatenate([handoff_a, handoff_b], axis=1)
+    k_grad, v_grad = stage(me, own_gradients, [bf16(tokens, KW)] * 2, summed, own)
+    handoff = jnp.concatenate([handoff_a, handoff_b, handoff_c], axis=1)
     return handoff[None, None], q_grad[None, None], k_grad[None, None], v_grad[None, None]
 
 

time: 142 us -> 140 us (0.986)
  the two profiles are of different devices: /device:TPU:65 before, /device:TPU:67 now
where the time goes in v4:
time: 140 us; the launch traced here: 139 us
  starting transfers between devices  58.6 us (42%)
  blocking collectives  37.2 us (27%)
  waiting for transfers between devices  22 us (16%)
  Pallas kernels  16.9 us (12%)
  other arithmetic  1.92 us (1%)
  local copies, waits for them, and re-layouts  1.57 us (1%)
    all_to_all x1, blocking collectives, own_gradients(): lax.all_to_all(summed.reshape(N_CTX, N_DP, BLOCK_POSITIONS, HEAD_SIZE), '...  23.7 us
    all_to_all x1, blocking collectives, sum_gradients(): lax.all_to_all(sends, 'ctx', 0, 0, tiled=True, axis_index_groups=halves)  13.5 us
    ppermute x3, waiting for transfers between devices, on_device(): lax.ppermute(payloads[at], 'dp', [(i, (i + at) % N_DP) for i in range(N_D...  11.4 us
    all_to_all x1, starting transfers between devices, on_device(): held = lax.all_to_all(pieces, ('dp', 'ctx'), 0, 0, tiled=True)  10.7 us
    ppermute x1, starting transfers between devices, on_device(): relay = lax.ppermute(attn_c, 'section', around)  9.75 us
    ppermute x3, starting transfers between devices, on_device(): lax.ppermute(payloads[at], 'dp', [(i, (i + at) % N_DP) for i in range(N_D...  9.16 us
    ppermute x1, starting transfers between devices, on_device(): relay = lax.ppermute(relay, 'section', around)  8 us
    ppermute x1, waiting for transfers between devices, on_device(): relay = lax.ppermute(attn_c, 'section', around)  6.39 us
  transfers between devices with their start and end apart: 11, of which 4 were waited for; matrix products, arithmetic and copies ran while one was open for 1% of the time, Pallas kernels for 8%

profile of v4, /device:TPU:67, one launch (start us, length us, event | category | flops | bytes accessed | tf_op | source)
XLA Modules:
  0.0 139.1 jit_solution(16815145247996675347)
XLA Ops:
  1.4 3.5 %shard_map.111 = (bf16[64,32,128]{2,1,0:T(8,128)(2,1)}, bf16[32,5120]{1,0:T(8,128)(2,1)}, bf16[32,5120]{1,0:T(8,128)(2,1)S(1)}, bf16[32,5120]{1,0:T(8,128)(2,1)S...) custom-call(s32[2]{0:T(128)S(1)} %pad_add_fusion.1.me, s32[4,4]{1,0:T(4,128)S(1)} %copy-done, ...), custom_call_target="tpu_custom_call" | custom-call | bytes 4718592 | tf_op jit(solution)/shard_map/pallas_call | solution.py:246
  5.0 10.7 %all-to-all-start.2 = ((bf16[64,32,128]{2,1,0:T(8,128)(2,1)}), bf16[64,32,128]{2,1,0:T(8,128)(2,1)S(1)}, u32[]{:S(2)}, u32[]{:S(2)}) async-start(bf16[64,32,128]{2,1,0:T(8,128)(2,1)} %get-tuple-element.71), calls=%async_computation.2 | async-start | bytes 1048576 | tf_op jit(solution)/shard_map/all_to_all | solution.py:255
  15.6 3.2 %collective-permute-start = (bf16[32,5120]{1,0:T(8,128)(2,1)S(1)}, bf16[32,5120]{1,0:T(8,128)(2,1)S(1)}, u32[]{:S(2)}, u32[]{:S(2)}) collective-permute-start(bf16[32,5120]{1,0:T(8,128)(2,1)S(1)} %get-tuple-element.68), channel_id=1, source_target_pairs={{0,128},{128,256},{256,384},{384,0},{1,129},{129,257},{257,385},{3... | collective-permute-start | bytes 983048 | tf_op jit(solution)/shard_map/ppermute | solution.py:258
  18.9 2.1 %collective-permute-start.2 = (bf16[32,5120]{1,0:T(8,128)(2,1)S(1)}, bf16[32,5120]{1,0:T(8,128)(2,1)S(1)}, u32[]{:S(2)}, u32[]{:S(2)}) collective-permute-start(bf16[32,5120]{1,0:T(8,128)(2,1)S(1)} %get-tuple-element.70), channel_id=1, source_target_pairs={{0,384},{128,0},{256,128},{384,256},{1,385},{129,1},{257,129},{385... | collective-permute-start | bytes 983048 | tf_op jit(solution)/shard_map/ppermute | solution.py:258
  20.9 8.9 %collective-permute-done.after.x1 = bf16[32,5120]{1,0:T(8,128)(2,1)S(1)} collective-permute-done((bf16[32,5120]{1,0:T(8,128)(2,1)S(1)}, bf16[32,5120]{1,0:T(8,128)(2,1)S(1)}, u32[]{:S(2)}, u32[]{:S(2)}) %collective-permute-start) | collective-permute-done | bytes 327712 | tf_op jit(solution)/shard_map/ppermute | solution.py:258
  29.9 2.5 %collective-permute-done.2.before.x3 = bf16[32,5120]{1,0:T(8,128)(2,1)S(1)} collective-permute-done((bf16[32,5120]{1,0:T(8,128)(2,1)S(1)}, bf16[32,5120]{1,0:T(8,128)(2,1)S(1)}, u32[]{:S(2)}, u32[]{:S(2)}) %collective-permute-start.2) | collective-permute-done | bytes 327712 | tf_op jit(solution)/shard_map/ppermute | solution.py:258
  32.3 1.8 %shard_map.112 = bf16[8,12,32,128]{3,2,1,0:T(8,128)(2,1)} custom-call(s32[2]{0:T(128)S(1)} %pad_add_fusion.1.me, s32[4,4]{1,0:T(4,128)S(1)} %copy-done.3, s32[64]{0:T(128)S(1)} %bitcast.27, bf16[64,32,128]{2,1,0:T(8,128)(2,1)S(1)} %all-to-all-done.2.held, bf16[32,5120]{1,0:T(8,128)(2,1)S(1)} %collective-permute-done.after.x1, ...), custom_call_target="tpu_custom_call" | custom-call | bytes 1048576 | tf_op jit(solution)/shard_map/pallas_call | solution.py:264
  34.1 4.3 %all-to-all-start.3 = ((bf16[8,12,32,128]{3,2,1,0:T(8,128)(2,1)}), bf16[8,12,32,128]{3,2,1,0:T(8,128)(2,1)S(1)}, u32[]{:S(2)}, u32[]{:S(2)}) async-start(bf16[8,12,32,128]{3,2,1,0:T(8,128)(2,1)} %shard_map.112), calls=%async_computation.3 | async-start | bytes 1572864 | tf_op jit(solution)/shard_map/all_to_all | solution.py:267
  38.3 3.9 %collective-permute-start.1 = (bf16[32,5120]{1,0:T(8,128)(2,1)S(1)}, bf16[32,5120]{1,0:T(8,128)(2,1)}, u32[]{:S(2)}, u32[]{:S(2)}) collective-permute-start(bf16[32,5120]{1,0:T(8,128)(2,1)S(1)} %get-tuple-element.69), channel_id=1, source_target_pairs={{0,256},{128,384},{256,0},{384,128},{1,257},{129,385},{257,1},{385... | collective-permute-start | bytes 983048 | tf_op jit(solution)/shard_map/ppermute | solution.py:258
  43.5 4.3 %all-to-all-done.3.win = bf16[8,12,32,128]{3,2,1,0:T(8,128)(2,1)S(1)} async-done(((bf16[8,12,32,128]{3,2,1,0:T(8,128)(2,1)}), bf16[8,12,32,128]{3,2,1,0:T(8,128)(2,1)S(1)}, u32[]{:S(2)}, u32[]{:S(2)}) %all-to-all-start.3) | async-done | bytes 786464 | tf_op jit(solution)/shard_map/all_to_all | solution.py:267
  47.7 4.8 %all-to-all-start.4 = ((bf16[4,32,4096]{2,1,0:T(8,128)(2,1)}), bf16[4,32,4096]{2,1,0:T(8,128)(2,1)}, u32[]{:S(2)}, u32[]{:S(2)}) async-start(bf16[4,32,4096]{2,1,0:T(8,128)(2,1)} %get-tuple-element.73), calls=%async_computation.4 | async-start | bytes 2097152 | tf_op jit(solution)/shard_map/all_to_all | solution.py:268
  53.0 3.3 %shard_map.113 = (bf16[128,2048]{1,0:T(8,128)(2,1)S(1)}, bf16[128,1024]{1,0:T(8,128)(2,1)S(1)}, bf16[128,1024]{1,0:T(8,128)(2,1)S(1)}, bf16[16,128,256]{2,1,0:T(8,128)(2,1)}) custom-call(s32[2]{0:T(128)S(1)} %pad_add_fusion.1.me, s32[4,4]{1,0:T(4,128)S(1)} %copy-done.3, s32[64]{0:T(128)S(1)} %bitcast.28, bf16[32,5120]{1,0:T(8,128)(2,1)S(1)} %copy-done.1, ...), custom_call_target="tpu_custom_call" | custom-call | flops 536870912 | bytes 6291456 | tf_op jit(solution)/shard_map/pallas_call | solution.py:270
  56.3 9.7 %collective-permute-start.4 = (bf16[128,1024]{1,0:T(8,128)(2,1)S(1)}, bf16[128,1024]{1,0:T(8,128)(2,1)}, u32[]{:S(2)}, u32[]{:S(2)}) collective-permute-start(bf16[128,1024]{1,0:T(8,128)(2,1)S(1)} %get-tuple-element.77), channel_id=1, source_target_pairs={{1,7},{3,1},{5,3},{7,5},{9,15},{11,9},{13,11},{15,13},{17,23},{19,... | collective-permute-start | bytes 786440 | tf_op jit(solution)/shard_map/ppermute | solution.py:283
  66.0 3.9 %collective-permute-start.3 = (bf16[128,2048]{1,0:T(8,128)(2,1)S(1)}, bf16[128,2048]{1,0:T(8,128)(2,1)S(1)}, u32[]{:S(2)}, u32[]{:S(2)}) collective-permute-start(bf16[128,2048]{1,0:T(8,128)(2,1)S(1)} %get-tuple-element.72), channel_id=1, source_target_pairs={{0,1},{1,2},{2,3},{3,4},{4,5},{5,6},{6,7},{7,0},{8,9},{9,10},{10,1... | collective-permute-start | bytes 1572872 | tf_op jit(solution)/shard_map/ppermute | solution.py:282
  69.9 6.4 %collective-permute-done.4 = bf16[128,1024]{1,0:T(8,128)(2,1)} collective-permute-done((bf16[128,1024]{1,0:T(8,128)(2,1)S(1)}, bf16[128,1024]{1,0:T(8,128)(2,1)}, u32[]{:S(2)}, u32[]{:S(2)}) %collective-permute-start.4) | collective-permute-done | bytes 262176 | tf_op jit(solution)/shard_map/ppermute | solution.py:283
  76.3 8.0 %collective-permute-start.5 = (bf16[128,1024]{1,0:T(8,128)(2,1)}, bf16[128,1024]{1,0:T(8,128)(2,1)S(1)}, u32[]{:S(2)}, u32[]{:S(2)}) collective-permute-start(bf16[128,1024]{1,0:T(8,128)(2,1)} %collective-permute-done.4), channel_id=1, source_target_pairs={{1,7},{3,1},{5,3},{7,5},{9,15},{11,9},{13,11},{15,13},{17,23},{19,... | collective-permute-start | bytes 786440 | tf_op jit(solution)/shard_map/ppermute | solution.py:284
  84.4 21.1 %conditional.2 = (bf16[64,32,128]{2,1,0:T(8,128)(2,1)S(1)}, f32[128,1024]{1,0:T(8,128)S(1)}, bf16[1,1,128,4096]{3,2,1,0:T(8,128)(2,1)}) conditional(s32[]{:T(128)} %convert_element_type.4, () %tuple.30, (s32[2]{0:T(128)S(1)}, s32[4,4]{1,0:T(4,128)S(1)}, bf16[32,5120]{1,0:T(8,128)(2,1)}, bf16[32,5120]{1,0:T(8,128)(2,1)S(1)}, ...), branch_computations={%region_0.0_spmd, %region_1.0_spmd} | conditional | flops 1073741824 | bytes 8912920 | solution.py:230
  84.4 6.2 %branch_1_fun.3 = (bf16[128,4096]{1,0:T(8,128)(2,1)}, bf16[8,12,32,128]{3,2,1,0:T(8,128)(2,1)S(1)}, f32[128,1024]{1,0:T(8,128)S(1)}) custom-call(s32[2]{0:T(128)S(1)} %get-tuple-element.29.me, s32[4,4]{1,0:T(4,128)S(1)} %get-tuple-element.30.recv, bf16[32,5120]{1,0:T(8,128)(2,1)} %get-tuple-element.32.x0, bf16[32,5120]{1,0:T(8,128)(2,1)S(1)} %get-tuple-element.33.x1, ...), custom_call_target="tpu_custom_call" | custom-call | flops 1073741824 | bytes 6291456 | tf_op jit(solution)/shard_map/cond/branch_1_fun/pallas_call | solution.py:287
  90.5 13.5 %all_to_all.23 = bf16[8,12,32,128]{3,2,1,0:T(8,128)(2,1)S(1)} all-to-all(bf16[8,12,32,128]{3,2,1,0:T(8,128)(2,1)S(1)} %get-tuple-element.39), channel_id=1, replica_groups={{0,8,16,24,32,40,48,56},{64,72,80,88,96,104,112,120},{1,9,17,25,33,41,4..., dimensions={0} | all-to-all | bytes 1572864 | tf_op jit(solution)/shard_map/cond/branch_1_fun/all_to_all | solution.py:294
  104.1 1.4 %branch_1_fun.4 = bf16[64,32,128]{2,1,0:T(8,128)(2,1)S(1)} custom-call(s32[2]{0:T(128)S(1)} %get-tuple-element.29.me, s32[4,4]{1,0:T(4,128)S(1)} %get-tuple-element.30.recv, s32[64]{0:T(128)S(1)} %get-tuple-element.31.stretch, bf16[96,32,128]{2,1,0:T(8,128)(2,1)S(1)} %bitcast.16), custom_call_target="tpu_custom_call" | custom-call | bytes 1048576 | tf_op jit(solution)/shard_map/cond/branch_1_fun/pallas_call | solution.py:295
  105.5 6.1 %collective-permute-start.7 = (bf16[128,1024]{1,0:T(8,128)(2,1)S(1)}, bf16[128,1024]{1,0:T(8,128)(2,1)S(1)}, u32[]{:S(2)}, u32[]{:S(2)}) collective-permute-start(bf16[128,1024]{1,0:T(8,128)(2,1)S(1)} %broadcast_select_fusion), channel_id=1, source_target_pairs={{1,6},{3,0},{5,2},{7,4},{0,1},{2,3},{4,5},{6,7},{9,14},{11,8},{13,... | collective-permute-start | bytes 786440 | tf_op jit(solution)/shard_map/ppermute | solution.py:313
  111.7 1.9 %collective-permute-start.6 = (bf16[128,1024]{1,0:T(8,128)(2,1)S(1)}, bf16[128,1024]{1,0:T(8,128)(2,1)S(1)}, u32[]{:S(2)}, u32[]{:S(2)}) collective-permute-start(bf16[128,1024]{1,0:T(8,128)(2,1)S(1)} %get-tuple-element.78), channel_id=1, source_target_pairs={{0,1},{1,2},{2,3},{3,4},{4,5},{5,6},{6,7},{7,0},{8,9},{9,10},{10,1... | collective-permute-start | bytes 786440 | tf_op jit(solution)/shard_map/ppermute | solution.py:311
  113.6 24.4 %conditional.3 = (bf16[1,1,128,512]{3,2,1,0:T(8,128)(2,1)}, bf16[1,1,128,512]{3,2,1,0:T(8,128)(2,1)}) conditional(s32[]{:T(128)} %convert_element_type.4, () %tuple.32, (bf16[64,32,128]{2,1,0:T(8,128)(2,1)S(1)}, f32[128,1024]{1,0:T(8,128)S(1)}) %tuple.33), branch_computations={%region_2.3_spmd, %region_3.4_spmd} | conditional | bytes 2097168 | solution.py:230
  113.6 23.7 %all_to_all.24 = bf16[16,4,32,128]{3,2,1,0:T(8,128)(2,1)S(1)} all-to-all(bf16[16,4,32,128]{3,2,1,0:T(8,128)(2,1)S(1)} %bitcast.18), channel_id=1, replica_groups=mesh['dp'=4,'ctx'=16,'section'=8] {'ctx'}, dimensions={0} | all-to-all | bytes 1048576 | tf_op jit(solution)/shard_map/cond/branch_1_fun/all_to_all | solution.py:316
  (30 shorter events, 4.3 us)
Async XLA Ops:
  0.7 0.7 copy-start
  4.9 27.4 %copy-start.3 = (s32[4,4]{1,0:T(4,128)S(1)}, s32[4,4]{1,0:T(4,128)}, u32[]{:S(2)}) copy-start(s32[4,4]{1,0:T(4,128)} %recv.3) | copy-start | bytes 196
  5.0 27.4 %copy-start.4 = (s32[1,1,64]{2,1,0:T(1,128)S(1)}, s32[1,1,64]{2,1,0:T(1,128)}, u32[]{:S(2)}) copy-start(s32[1,1,64]{2,1,0:T(1,128)} %param.18) | copy-start | bytes 772
  5.0 27.3 %all-to-all-start.2 = ((bf16[64,32,128]{2,1,0:T(8,128)(2,1)}), bf16[64,32,128]{2,1,0:T(8,128)(2,1)S(1)}, u32[]{:S(2)}, u32[]{:S(2)}) async-start(bf16[64,32,128]{2,1,0:T(8,128)(2,1)} %get-tuple-element.71), calls=%async_computation.2 | async-start | bytes 1048576 | tf_op jit(solution)/shard_map/all_to_all | solution.py:255
  15.6 14.2 %collective-permute-start = (bf16[32,5120]{1,0:T(8,128)(2,1)S(1)}, bf16[32,5120]{1,0:T(8,128)(2,1)S(1)}, u32[]{:S(2)}, u32[]{:S(2)}) collective-permute-start(bf16[32,5120]{1,0:T(8,128)(2,1)S(1)} %get-tuple-element.68), channel_id=1, source_target_pairs={{0,128},{128,256},{256,384},{384,0},{1,129},{129,257},{257,385},{3... | collective-permute-start | bytes 983048 | tf_op jit(solution)/shard_map/ppermute | solution.py:258
  18.9 13.4 %collective-permute-start.2 = (bf16[32,5120]{1,0:T(8,128)(2,1)S(1)}, bf16[32,5120]{1,0:T(8,128)(2,1)S(1)}, u32[]{:S(2)}, u32[]{:S(2)}) collective-permute-start(bf16[32,5120]{1,0:T(8,128)(2,1)S(1)} %get-tuple-element.70), channel_id=1, source_target_pairs={{0,384},{128,0},{256,128},{384,256},{1,385},{129,1},{257,129},{385... | collective-permute-start | bytes 983048 | tf_op jit(solution)/shard_map/ppermute | solution.py:258
  34.1 8.7 %copy-start.2 = (s32[1,1,2048]{2,1,0:T(1,128)S(1)}, s32[1,1,2048]{2,1,0:T(1,128)}, u32[]{:S(2)}) copy-start(s32[1,1,2048]{2,1,0:T(1,128)} %param.19) | copy-start | bytes 24580
  34.1 13.7 %all-to-all-start.3 = ((bf16[8,12,32,128]{3,2,1,0:T(8,128)(2,1)}), bf16[8,12,32,128]{3,2,1,0:T(8,128)(2,1)S(1)}, u32[]{:S(2)}, u32[]{:S(2)}) async-start(bf16[8,12,32,128]{3,2,1,0:T(8,128)(2,1)} %shard_map.112), calls=%async_computation.3 | async-start | bytes 1572864 | tf_op jit(solution)/shard_map/all_to_all | solution.py:267
  38.3 14.6 %collective-permute-start.1 = (bf16[32,5120]{1,0:T(8,128)(2,1)S(1)}, bf16[32,5120]{1,0:T(8,128)(2,1)}, u32[]{:S(2)}, u32[]{:S(2)}) collective-permute-start(bf16[32,5120]{1,0:T(8,128)(2,1)S(1)} %get-tuple-element.69), channel_id=1, source_target_pairs={{0,256},{128,384},{256,0},{384,128},{1,257},{129,385},{257,1},{385... | collective-permute-start | bytes 983048 | tf_op jit(solution)/shard_map/ppermute | solution.py:258
  47.7 5.2 %copy-start.1 = (bf16[32,5120]{1,0:T(8,128)(2,1)S(1)}, bf16[32,5120]{1,0:T(8,128)(2,1)}, u32[]{:S(2)}) copy-start(bf16[32,5120]{1,0:T(8,128)(2,1)} %get-tuple-element.67.x0) | copy-start | bytes 983044
  47.7 36.6 %all-to-all-start.4 = ((bf16[4,32,4096]{2,1,0:T(8,128)(2,1)}), bf16[4,32,4096]{2,1,0:T(8,128)(2,1)}, u32[]{:S(2)}, u32[]{:S(2)}) async-start(bf16[4,32,4096]{2,1,0:T(8,128)(2,1)} %get-tuple-element.73), calls=%async_computation.4 | async-start | bytes 2097152 | tf_op jit(solution)/shard_map/all_to_all | solution.py:268
  56.3 20.0 %collective-permute-start.4 = (bf16[128,1024]{1,0:T(8,128)(2,1)S(1)}, bf16[128,1024]{1,0:T(8,128)(2,1)}, u32[]{:S(2)}, u32[]{:S(2)}) collective-permute-start(bf16[128,1024]{1,0:T(8,128)(2,1)S(1)} %get-tuple-element.77), channel_id=1, source_target_pairs={{1,7},{3,1},{5,3},{7,5},{9,15},{11,9},{13,11},{15,13},{17,23},{19,... | collective-permute-start | bytes 786440 | tf_op jit(solution)/shard_map/ppermute | solution.py:283
  66.0 45.6 %collective-permute-start.3 = (bf16[128,2048]{1,0:T(8,128)(2,1)S(1)}, bf16[128,2048]{1,0:T(8,128)(2,1)S(1)}, u32[]{:S(2)}, u32[]{:S(2)}) collective-permute-start(bf16[128,2048]{1,0:T(8,128)(2,1)S(1)} %get-tuple-element.72), channel_id=1, source_target_pairs={{0,1},{1,2},{2,3},{3,4},{4,5},{5,6},{6,7},{7,0},{8,9},{9,10},{10,1... | collective-permute-start | bytes 1572872 | tf_op jit(solution)/shard_map/ppermute | solution.py:282
  76.3 29.2 %collective-permute-start.5 = (bf16[128,1024]{1,0:T(8,128)(2,1)}, bf16[128,1024]{1,0:T(8,128)(2,1)S(1)}, u32[]{:S(2)}, u32[]{:S(2)}) collective-permute-start(bf16[128,1024]{1,0:T(8,128)(2,1)} %collective-permute-done.4), channel_id=1, source_target_pairs={{1,7},{3,1},{5,3},{7,5},{9,15},{11,9},{13,11},{15,13},{17,23},{19,... | collective-permute-start | bytes 786440 | tf_op jit(solution)/shard_map/ppermute | solution.py:284
  105.5 32.5 %collective-permute-start.7 = (bf16[128,1024]{1,0:T(8,128)(2,1)S(1)}, bf16[128,1024]{1,0:T(8,128)(2,1)S(1)}, u32[]{:S(2)}, u32[]{:S(2)}) collective-permute-start(bf16[128,1024]{1,0:T(8,128)(2,1)S(1)} %broadcast_select_fusion), channel_id=1, source_target_pairs={{1,6},{3,0},{5,2},{7,4},{0,1},{2,3},{4,5},{6,7},{9,14},{11,8},{13,... | collective-permute-start | bytes 786440 | tf_op jit(solution)/shard_map/ppermute | solution.py:313
  111.7 26.4 %collective-permute-start.6 = (bf16[128,1024]{1,0:T(8,128)(2,1)S(1)}, bf16[128,1024]{1,0:T(8,128)(2,1)S(1)}, u32[]{:S(2)}, u32[]{:S(2)}) collective-permute-start(bf16[128,1024]{1,0:T(8,128)(2,1)S(1)} %get-tuple-element.78), channel_id=1, source_target_pairs={{0,1},{1,2},{2,3},{3,4},{4,5},{5,6},{6,7},{7,0},{8,9},{9,10},{10,1... | collective-permute-start | bytes 786440 | tf_op jit(solution)/shard_map/ppermute | solution.py:311

commit v5 on v4

--- a/solution.py
+++ b/solution.py
@@ -35,7 +35,7 @@
 
 
 def call(
-    kernel, out_shape, in_specs, scratch=(), flops=0, nbytes=1 << 20, out_space=VMEM, aliases={}, limit=40
+    kernel, out_shape, in_specs, scratch=(), flops=0, nbytes=1 << 20, out_space=VMEM, aliases={}, limit=20
 ):
     if isinstance(out_shape, list) and not isinstance(out_space, list):
         out_space = [out_space] * len(out_shape)

time: 140 us -> 140 us (level)
  no operation moved by 1% of the time
where the time goes in v5:
time: 140 us; the launch traced here: 139 us
  starting transfers between devices  58.6 us (42%)
  blocking collectives  37.2 us (27%)
  waiting for transfers between devices  22 us (16%)
  Pallas kernels  16.9 us (12%)
  other arithmetic  1.92 us (1%)
  local copies, waits for them, and re-layouts  1.57 us (1%)
    all_to_all x1, blocking collectives, own_gradients(): lax.all_to_all(summed.reshape(N_CTX, N_DP, BLOCK_POSITIONS, HEAD_SIZE), '...  23.7 us
    all_to_all x1, blocking collectives, sum_gradients(): lax.all_to_all(sends, 'ctx', 0, 0, tiled=True, axis_index_groups=halves)  13.6 us
    ppermute x3, waiting for transfers between devices, on_device(): lax.ppermute(payloads[at], 'dp', [(i, (i + at) % N_DP) for i in range(N_D...  11.4 us
    all_to_all x1, starting transfers between devices, on_device(): held = lax.all_to_all(pieces, ('dp', 'ctx'), 0, 0, tiled=True)  10.7 us
    ppermute x1, starting transfers between devices, on_device(): relay = lax.ppermute(attn_c, 'section', around)  9.75 us
    ppermute x3, starting transfers between devices, on_device(): lax.ppermute(payloads[at], 'dp', [(i, (i + at) % N_DP) for i in range(N_D...  9.16 us
    ppermute x1, starting transfers between devices, on_device(): relay = lax.ppermute(relay, 'section', around)  8 us
    ppermute x1, waiting for transfers between devices, on_device(): relay = lax.ppermute(attn_c, 'section', around)  6.39 us
  transfers between devices with their start and end apart: 11, of which 4 were waited for; matrix products, arithmetic and copies ran while one was open for 1% of the time, Pallas kernels for 8%

profile of v5, /device:TPU:67, one launch (start us, length us, event | category | flops | bytes accessed | tf_op | source)
XLA Modules:
  0.0 139.1 jit_solution(15478283116225134739)
XLA Ops:
  1.4 3.5 %shard_map.111 = (bf16[64,32,128]{2,1,0:T(8,128)(2,1)}, bf16[32,5120]{1,0:T(8,128)(2,1)}, bf16[32,5120]{1,0:T(8,128)(2,1)S(1)}, bf16[32,5120]{1,0:T(8,128)(2,1)S...) custom-call(s32[2]{0:T(128)S(1)} %pad_add_fusion.1.me, s32[4,4]{1,0:T(4,128)S(1)} %copy-done, ...), custom_call_target="tpu_custom_call" | custom-call | bytes 4718592 | tf_op jit(solution)/shard_map/pallas_call | solution.py:246
  5.0 10.7 %all-to-all-start.2 = ((bf16[64,32,128]{2,1,0:T(8,128)(2,1)}), bf16[64,32,128]{2,1,0:T(8,128)(2,1)S(1)}, u32[]{:S(2)}, u32[]{:S(2)}) async-start(bf16[64,32,128]{2,1,0:T(8,128)(2,1)} %get-tuple-element.71), calls=%async_computation.2 | async-start | bytes 1048576 | tf_op jit(solution)/shard_map/all_to_all | solution.py:255
  15.6 3.2 %collective-permute-start = (bf16[32,5120]{1,0:T(8,128)(2,1)S(1)}, bf16[32,5120]{1,0:T(8,128)(2,1)S(1)}, u32[]{:S(2)}, u32[]{:S(2)}) collective-permute-start(bf16[32,5120]{1,0:T(8,128)(2,1)S(1)} %get-tuple-element.68), channel_id=1, source_target_pairs={{0,128},{128,256},{256,384},{384,0},{1,129},{129,257},{257,385},{3... | collective-permute-start | bytes 983048 | tf_op jit(solution)/shard_map/ppermute | solution.py:258
  18.9 2.1 %collective-permute-start.2 = (bf16[32,5120]{1,0:T(8,128)(2,1)S(1)}, bf16[32,5120]{1,0:T(8,128)(2,1)S(1)}, u32[]{:S(2)}, u32[]{:S(2)}) collective-permute-start(bf16[32,5120]{1,0:T(8,128)(2,1)S(1)} %get-tuple-element.70), channel_id=1, source_target_pairs={{0,384},{128,0},{256,128},{384,256},{1,385},{129,1},{257,129},{385... | collective-permute-start | bytes 983048 | tf_op jit(solution)/shard_map/ppermute | solution.py:258
  20.9 8.9 %collective-permute-done.after.x1 = bf16[32,5120]{1,0:T(8,128)(2,1)S(1)} collective-permute-done((bf16[32,5120]{1,0:T(8,128)(2,1)S(1)}, bf16[32,5120]{1,0:T(8,128)(2,1)S(1)}, u32[]{:S(2)}, u32[]{:S(2)}) %collective-permute-start) | collective-permute-done | bytes 327712 | tf_op jit(solution)/shard_map/ppermute | solution.py:258
  29.9 2.5 %collective-permute-done.2.before.x3 = bf16[32,5120]{1,0:T(8,128)(2,1)S(1)} collective-permute-done((bf16[32,5120]{1,0:T(8,128)(2,1)S(1)}, bf16[32,5120]{1,0:T(8,128)(2,1)S(1)}, u32[]{:S(2)}, u32[]{:S(2)}) %collective-permute-start.2) | collective-permute-done | bytes 327712 | tf_op jit(solution)/shard_map/ppermute | solution.py:258
  32.3 1.8 %shard_map.112 = bf16[8,12,32,128]{3,2,1,0:T(8,128)(2,1)} custom-call(s32[2]{0:T(128)S(1)} %pad_add_fusion.1.me, s32[4,4]{1,0:T(4,128)S(1)} %copy-done.3, s32[64]{0:T(128)S(1)} %bitcast.27, bf16[64,32,128]{2,1,0:T(8,128)(2,1)S(1)} %all-to-all-done.2.held, bf16[32,5120]{1,0:T(8,128)(2,1)S(1)} %collective-permute-done.after.x1, ...), custom_call_target="tpu_custom_call" | custom-call | bytes 1048576 | tf_op jit(solution)/shard_map/pallas_call | solution.py:264
  34.1 4.3 %all-to-all-start.3 = ((bf16[8,12,32,128]{3,2,1,0:T(8,128)(2,1)}), bf16[8,12,32,128]{3,2,1,0:T(8,128)(2,1)S(1)}, u32[]{:S(2)}, u32[]{:S(2)}) async-start(bf16[8,12,32,128]{3,2,1,0:T(8,128)(2,1)} %shard_map.112), calls=%async_computation.3 | async-start | bytes 1572864 | tf_op jit(solution)/shard_map/all_to_all | solution.py:267
  38.3 3.9 %collective-permute-start.1 = (bf16[32,5120]{1,0:T(8,128)(2,1)S(1)}, bf16[32,5120]{1,0:T(8,128)(2,1)}, u32[]{:S(2)}, u32[]{:S(2)}) collective-permute-start(bf16[32,5120]{1,0:T(8,128)(2,1)S(1)} %get-tuple-element.69), channel_id=1, source_target_pairs={{0,256},{128,384},{256,0},{384,128},{1,257},{129,385},{257,1},{385... | collective-permute-start | bytes 983048 | tf_op jit(solution)/shard_map/ppermute | solution.py:258
  43.5 4.3 %all-to-all-done.3.win = bf16[8,12,32,128]{3,2,1,0:T(8,128)(2,1)S(1)} async-done(((bf16[8,12,32,128]{3,2,1,0:T(8,128)(2,1)}), bf16[8,12,32,128]{3,2,1,0:T(8,128)(2,1)S(1)}, u32[]{:S(2)}, u32[]{:S(2)}) %all-to-all-start.3) | async-done | bytes 786464 | tf_op jit(solution)/shard_map/all_to_all | solution.py:267
  47.7 4.8 %all-to-all-start.4 = ((bf16[4,32,4096]{2,1,0:T(8,128)(2,1)}), bf16[4,32,4096]{2,1,0:T(8,128)(2,1)}, u32[]{:S(2)}, u32[]{:S(2)}) async-start(bf16[4,32,4096]{2,1,0:T(8,128)(2,1)} %get-tuple-element.73), calls=%async_computation.4 | async-start | bytes 2097152 | tf_op jit(solution)/shard_map/all_to_all | solution.py:268
  53.0 3.3 %shard_map.113 = (bf16[128,2048]{1,0:T(8,128)(2,1)S(1)}, bf16[128,1024]{1,0:T(8,128)(2,1)S(1)}, bf16[128,1024]{1,0:T(8,128)(2,1)S(1)}, bf16[16,128,256]{2,1,0:T(8,128)(2,1)}) custom-call(s32[2]{0:T(128)S(1)} %pad_add_fusion.1.me, s32[4,4]{1,0:T(4,128)S(1)} %copy-done.3, s32[64]{0:T(128)S(1)} %bitcast.28, bf16[32,5120]{1,0:T(8,128)(2,1)S(1)} %copy-done.1, ...), custom_call_target="tpu_custom_call" | custom-call | flops 536870912 | bytes 6291456 | tf_op jit(solution)/shard_map/pallas_call | solution.py:270
  56.3 9.7 %collective-permute-start.4 = (bf16[128,1024]{1,0:T(8,128)(2,1)S(1)}, bf16[128,1024]{1,0:T(8,128)(2,1)}, u32[]{:S(2)}, u32[]{:S(2)}) collective-permute-start(bf16[128,1024]{1,0:T(8,128)(2,1)S(1)} %get-tuple-element.77), channel_id=1, source_target_pairs={{1,7},{3,1},{5,3},{7,5},{9,15},{11,9},{13,11},{15,13},{17,23},{19,... | collective-permute-start | bytes 786440 | tf_op jit(solution)/shard_map/ppermute | solution.py:283
  66.0 3.9 %collective-permute-start.3 = (bf16[128,2048]{1,0:T(8,128)(2,1)S(1)}, bf16[128,2048]{1,0:T(8,128)(2,1)S(1)}, u32[]{:S(2)}, u32[]{:S(2)}) collective-permute-start(bf16[128,2048]{1,0:T(8,128)(2,1)S(1)} %get-tuple-element.72), channel_id=1, source_target_pairs={{0,1},{1,2},{2,3},{3,4},{4,5},{5,6},{6,7},{7,0},{8,9},{9,10},{10,1... | collective-permute-start | bytes 1572872 | tf_op jit(solution)/shard_map/ppermute | solution.py:282
  69.9 6.4 %collective-permute-done.4 = bf16[128,1024]{1,0:T(8,128)(2,1)} collective-permute-done((bf16[128,1024]{1,0:T(8,128)(2,1)S(1)}, bf16[128,1024]{1,0:T(8,128)(2,1)}, u32[]{:S(2)}, u32[]{:S(2)}) %collective-permute-start.4) | collective-permute-done | bytes 262176 | tf_op jit(solution)/shard_map/ppermute | solution.py:283
  76.3 8.0 %collective-permute-start.5 = (bf16[128,1024]{1,0:T(8,128)(2,1)}, bf16[128,1024]{1,0:T(8,128)(2,1)S(1)}, u32[]{:S(2)}, u32[]{:S(2)}) collective-permute-start(bf16[128,1024]{1,0:T(8,128)(2,1)} %collective-permute-done.4), channel_id=1, source_target_pairs={{1,7},{3,1},{5,3},{7,5},{9,15},{11,9},{13,11},{15,13},{17,23},{19,... | collective-permute-start | bytes 786440 | tf_op jit(solution)/shard_map/ppermute | solution.py:284
  84.4 21.1 %conditional.2 = (bf16[64,32,128]{2,1,0:T(8,128)(2,1)S(1)}, f32[128,1024]{1,0:T(8,128)S(1)}, bf16[1,1,128,4096]{3,2,1,0:T(8,128)(2,1)}) conditional(s32[]{:T(128)} %convert_element_type.4, () %tuple.30, (s32[2]{0:T(128)S(1)}, s32[4,4]{1,0:T(4,128)S(1)}, bf16[32,5120]{1,0:T(8,128)(2,1)}, bf16[32,5120]{1,0:T(8,128)(2,1)S(1)}, ...), branch_computations={%region_0.0_spmd, %region_1.0_spmd} | conditional | flops 1073741824 | bytes 8912920 | solution.py:230
  84.4 6.2 %branch_1_fun.3 = (bf16[128,4096]{1,0:T(8,128)(2,1)}, bf16[8,12,32,128]{3,2,1,0:T(8,128)(2,1)S(1)}, f32[128,1024]{1,0:T(8,128)S(1)}) custom-call(s32[2]{0:T(128)S(1)} %get-tuple-element.29.me, s32[4,4]{1,0:T(4,128)S(1)} %get-tuple-element.30.recv, bf16[32,5120]{1,0:T(8,128)(2,1)} %get-tuple-element.32.x0, bf16[32,5120]{1,0:T(8,128)(2,1)S(1)} %get-tuple-element.33.x1, ...), custom_call_target="tpu_custom_call" | custom-call | flops 1073741824 | bytes 6291456 | tf_op jit(solution)/shard_map/cond/branch_1_fun/pallas_call | solution.py:287
  90.5 13.6 %all_to_all.23 = bf16[8,12,32,128]{3,2,1,0:T(8,128)(2,1)S(1)} all-to-all(bf16[8,12,32,128]{3,2,1,0:T(8,128)(2,1)S(1)} %get-tuple-element.39), channel_id=1, replica_groups={{0,8,16,24,32,40,48,56},{64,72,80,88,96,104,112,120},{1,9,17,25,33,41,4..., dimensions={0} | all-to-all | bytes 1572864 | tf_op jit(solution)/shard_map/cond/branch_1_fun/all_to_all | solution.py:294
  104.1 1.4 %branch_1_fun.4 = bf16[64,32,128]{2,1,0:T(8,128)(2,1)S(1)} custom-call(s32[2]{0:T(128)S(1)} %get-tuple-element.29.me, s32[4,4]{1,0:T(4,128)S(1)} %get-tuple-element.30.recv, s32[64]{0:T(128)S(1)} %get-tuple-element.31.stretch, bf16[96,32,128]{2,1,0:T(8,128)(2,1)S(1)} %bitcast.16), custom_call_target="tpu_custom_call" | custom-call | bytes 1048576 | tf_op jit(solution)/shard_map/cond/branch_1_fun/pallas_call | solution.py:295
  105.6 6.1 %collective-permute-start.7 = (bf16[128,1024]{1,0:T(8,128)(2,1)S(1)}, bf16[128,1024]{1,0:T(8,128)(2,1)S(1)}, u32[]{:S(2)}, u32[]{:S(2)}) collective-permute-start(bf16[128,1024]{1,0:T(8,128)(2,1)S(1)} %broadcast_select_fusion), channel_id=1, source_target_pairs={{1,6},{3,0},{5,2},{7,4},{0,1},{2,3},{4,5},{6,7},{9,14},{11,8},{13,... | collective-permute-start | bytes 786440 | tf_op jit(solution)/shard_map/ppermute | solution.py:313
  111.7 1.9 %collective-permute-start.6 = (bf16[128,1024]{1,0:T(8,128)(2,1)S(1)}, bf16[128,1024]{1,0:T(8,128)(2,1)S(1)}, u32[]{:S(2)}, u32[]{:S(2)}) collective-permute-start(bf16[128,1024]{1,0:T(8,128)(2,1)S(1)} %get-tuple-element.78), channel_id=1, source_target_pairs={{0,1},{1,2},{2,3},{3,4},{4,5},{5,6},{6,7},{7,0},{8,9},{9,10},{10,1... | collective-permute-start | bytes 786440 | tf_op jit(solution)/shard_map/ppermute | solution.py:311
  113.6 24.4 %conditional.3 = (bf16[1,1,128,512]{3,2,1,0:T(8,128)(2,1)}, bf16[1,1,128,512]{3,2,1,0:T(8,128)(2,1)}) conditional(s32[]{:T(128)} %convert_element_type.4, () %tuple.32, (bf16[64,32,128]{2,1,0:T(8,128)(2,1)S(1)}, f32[128,1024]{1,0:T(8,128)S(1)}) %tuple.33), branch_computations={%region_2.3_spmd, %region_3.4_spmd} | conditional | bytes 2097168 | solution.py:230
  113.6 23.7 %all_to_all.24 = bf16[16,4,32,128]{3,2,1,0:T(8,128)(2,1)S(1)} all-to-all(bf16[16,4,32,128]{3,2,1,0:T(8,128)(2,1)S(1)} %bitcast.18), channel_id=1, replica_groups=mesh['dp'=4,'ctx'=16,'section'=8] {'ctx'}, dimensions={0} | all-to-all | bytes 1048576 | tf_op jit(solution)/shard_map/cond/branch_1_fun/all_to_all | solution.py:316
  (30 shorter events, 4.3 us)
Async XLA Ops:
  0.7 0.7 copy-start
  4.9 27.4 %copy-start.3 = (s32[4,4]{1,0:T(4,128)S(1)}, s32[4,4]{1,0:T(4,128)}, u32[]{:S(2)}) copy-start(s32[4,4]{1,0:T(4,128)} %recv.3) | copy-start | bytes 196
  5.0 27.4 %copy-start.4 = (s32[1,1,64]{2,1,0:T(1,128)S(1)}, s32[1,1,64]{2,1,0:T(1,128)}, u32[]{:S(2)}) copy-start(s32[1,1,64]{2,1,0:T(1,128)} %param.18) | copy-start | bytes 772
  5.0 27.3 %all-to-all-start.2 = ((bf16[64,32,128]{2,1,0:T(8,128)(2,1)}), bf16[64,32,128]{2,1,0:T(8,128)(2,1)S(1)}, u32[]{:S(2)}, u32[]{:S(2)}) async-start(bf16[64,32,128]{2,1,0:T(8,128)(2,1)} %get-tuple-element.71), calls=%async_computation.2 | async-start | bytes 1048576 | tf_op jit(solution)/shard_map/all_to_all | solution.py:255
  15.6 14.2 %collective-permute-start = (bf16[32,5120]{1,0:T(8,128)(2,1)S(1)}, bf16[32,5120]{1,0:T(8,128)(2,1)S(1)}, u32[]{:S(2)}, u32[]{:S(2)}) collective-permute-start(bf16[32,5120]{1,0:T(8,128)(2,1)S(1)} %get-tuple-element.68), channel_id=1, source_target_pairs={{0,128},{128,256},{256,384},{384,0},{1,129},{129,257},{257,385},{3... | collective-permute-start | bytes 983048 | tf_op jit(solution)/shard_map/ppermute | solution.py:258
  18.9 13.4 %collective-permute-start.2 = (bf16[32,5120]{1,0:T(8,128)(2,1)S(1)}, bf16[32,5120]{1,0:T(8,128)(2,1)S(1)}, u32[]{:S(2)}, u32[]{:S(2)}) collective-permute-start(bf16[32,5120]{1,0:T(8,128)(2,1)S(1)} %get-tuple-element.70), channel_id=1, source_target_pairs={{0,384},{128,0},{256,128},{384,256},{1,385},{129,1},{257,129},{385... | collective-permute-start | bytes 983048 | tf_op jit(solution)/shard_map/ppermute | solution.py:258
  34.1 8.7 %copy-start.2 = (s32[1,1,2048]{2,1,0:T(1,128)S(1)}, s32[1,1,2048]{2,1,0:T(1,128)}, u32[]{:S(2)}) copy-start(s32[1,1,2048]{2,1,0:T(1,128)} %param.19) | copy-start | bytes 24580
  34.1 13.7 %all-to-all-start.3 = ((bf16[8,12,32,128]{3,2,1,0:T(8,128)(2,1)}), bf16[8,12,32,128]{3,2,1,0:T(8,128)(2,1)S(1)}, u32[]{:S(2)}, u32[]{:S(2)}) async-start(bf16[8,12,32,128]{3,2,1,0:T(8,128)(2,1)} %shard_map.112), calls=%async_computation.3 | async-start | bytes 1572864 | tf_op jit(solution)/shard_map/all_to_all | solution.py:267
  38.3 14.6 %collective-permute-start.1 = (bf16[32,5120]{1,0:T(8,128)(2,1)S(1)}, bf16[32,5120]{1,0:T(8,128)(2,1)}, u32[]{:S(2)}, u32[]{:S(2)}) collective-permute-start(bf16[32,5120]{1,0:T(8,128)(2,1)S(1)} %get-tuple-element.69), channel_id=1, source_target_pairs={{0,256},{128,384},{256,0},{384,128},{1,257},{129,385},{257,1},{385... | collective-permute-start | bytes 983048 | tf_op jit(solution)/shard_map/ppermute | solution.py:258
  47.7 5.2 %copy-start.1 = (bf16[32,5120]{1,0:T(8,128)(2,1)S(1)}, bf16[32,5120]{1,0:T(8,128)(2,1)}, u32[]{:S(2)}) copy-start(bf16[32,5120]{1,0:T(8,128)(2,1)} %get-tuple-element.67.x0) | copy-start | bytes 983044
  47.7 36.6 %all-to-all-start.4 = ((bf16[4,32,4096]{2,1,0:T(8,128)(2,1)}), bf16[4,32,4096]{2,1,0:T(8,128)(2,1)}, u32[]{:S(2)}, u32[]{:S(2)}) async-start(bf16[4,32,4096]{2,1,0:T(8,128)(2,1)} %get-tuple-element.73), calls=%async_computation.4 | async-start | bytes 2097152 | tf_op jit(solution)/shard_map/all_to_all | solution.py:268
  56.3 20.0 %collective-permute-start.4 = (bf16[128,1024]{1,0:T(8,128)(2,1)S(1)}, bf16[128,1024]{1,0:T(8,128)(2,1)}, u32[]{:S(2)}, u32[]{:S(2)}) collective-permute-start(bf16[128,1024]{1,0:T(8,128)(2,1)S(1)} %get-tuple-element.77), channel_id=1, source_target_pairs={{1,7},{3,1},{5,3},{7,5},{9,15},{11,9},{13,11},{15,13},{17,23},{19,... | collective-permute-start | bytes 786440 | tf_op jit(solution)/shard_map/ppermute | solution.py:283
  66.0 45.6 %collective-permute-start.3 = (bf16[128,2048]{1,0:T(8,128)(2,1)S(1)}, bf16[128,2048]{1,0:T(8,128)(2,1)S(1)}, u32[]{:S(2)}, u32[]{:S(2)}) collective-permute-start(bf16[128,2048]{1,0:T(8,128)(2,1)S(1)} %get-tuple-element.72), channel_id=1, source_target_pairs={{0,1},{1,2},{2,3},{3,4},{4,5},{5,6},{6,7},{7,0},{8,9},{9,10},{10,1... | collective-permute-start | bytes 1572872 | tf_op jit(solution)/shard_map/ppermute | solution.py:282
  76.3 29.2 %collective-permute-start.5 = (bf16[128,1024]{1,0:T(8,128)(2,1)}, bf16[128,1024]{1,0:T(8,128)(2,1)S(1)}, u32[]{:S(2)}, u32[]{:S(2)}) collective-permute-start(bf16[128,1024]{1,0:T(8,128)(2,1)} %collective-permute-done.4), channel_id=1, source_target_pairs={{1,7},{3,1},{5,3},{7,5},{9,15},{11,9},{13,11},{15,13},{17,23},{19,... | collective-permute-start | bytes 786440 | tf_op jit(solution)/shard_map/ppermute | solution.py:284
  105.6 32.5 %collective-permute-start.7 = (bf16[128,1024]{1,0:T(8,128)(2,1)S(1)}, bf16[128,1024]{1,0:T(8,128)(2,1)S(1)}, u32[]{:S(2)}, u32[]{:S(2)}) collective-permute-start(bf16[128,1024]{1,0:T(8,128)(2,1)S(1)} %broadcast_select_fusion), channel_id=1, source_target_pairs={{1,6},{3,0},{5,2},{7,4},{0,1},{2,3},{4,5},{6,7},{9,14},{11,8},{13,... | collective-permute-start | bytes 786440 | tf_op jit(solution)/shard_map/ppermute | solution.py:313
  111.7 26.3 %collective-permute-start.6 = (bf16[128,1024]{1,0:T(8,128)(2,1)S(1)}, bf16[128,1024]{1,0:T(8,128)(2,1)S(1)}, u32[]{:S(2)}, u32[]{:S(2)}) collective-permute-start(bf16[128,1024]{1,0:T(8,128)(2,1)S(1)} %get-tuple-element.78), channel_id=1, source_target_pairs={{0,1},{1,2},{2,3},{3,4},{4,5},{5,6},{6,7},{7,0},{8,9},{9,10},{10,1... | collective-permute-start | bytes 786440 | tf_op jit(solution)/shard_map/ppermute | solution.py:311
